TPU v7x, 32 devices: a whole 2x2x4 slice. The times are simulated.
32 devices in a mesh: worker: 8 (over y, x, core), shard: 4 (over z).
Axes of the slice: x: 2, y: 2, z: 4, core: 2. Of those that a mesh axis runs over, the one named last changes fastest.
Arguments:
- momentum: float32 [8, 2097152], P('worker', 'shard'), may hold values from -6 to 6
- gradient: float32 [8, 2097152], P('worker', 'shard'), may hold values from -40 to 40
- weights: float32 [2097152], P('shard'), may hold values from -0.6 to 0.6
Outputs:
- new_momentum: float32 [8, 2097152], P('worker', 'shard')
- new_weights: float32 [2097152], P('shard')
All inputs are finite; a program needn't handle non-finite values.
Results may differ from a plain program's by a relative error of at most 0.0003.
Values sent between devices are 32-bit elements; how exact they have to be, the bound alone decides.
No kernel may reach another device: no remote copies, remote signals or barrier semaphores. Data moves between devices by JAX's collectives and lax.ppermute only.
A program may use at most 64 MiB of HBM per device.

v0:
```python
import jax
import jax.numpy as jnp
from jax import lax
from jax.sharding import PartitionSpec as P


def order_pairs(stacked):
    former = stacked[0::2]
    latter = stacked[1::2]
    paired = jnp.stack([jnp.minimum(former, latter), jnp.maximum(former, latter)], 1)
    return paired.reshape(stacked.shape)


def trimmed_mean(values):
    members = values.shape[0]
    trim_count = members // 4

    def one_round(step_index, current):
        current = order_pairs(current)
        middle = order_pairs(current[1 : members - 1])
        return jnp.concatenate([current[:1], middle, current[members - 1 :]], 0)

    ordered = lax.fori_loop(0, members // 2, one_round, values)
    kept = ordered[trim_count : members - trim_count]
    return jnp.sum(kept, axis=0) / (members - 2 * trim_count)


def body(momentum, gradient, weights):
    updated = 0.9 * momentum + gradient
    shard_len = updated.shape[1]
    workers_here = lax.axis_size("worker")
    block_len = shard_len // workers_here
    blocks = updated.reshape(workers_here, block_len // 128, 128)
    trimmed = trimmed_mean(
        lax.all_to_all(blocks, "worker", split_axis=0, concat_axis=0, tiled=True)
    )
    start = lax.axis_index("worker") * block_len
    own_weights = lax.dynamic_slice_in_dim(weights, start, block_len)
    own_new = own_weights - 0.1 * trimmed.reshape(block_len)
    new_weights = lax.all_gather(own_new, "worker", axis=0, tiled=True)
    return (updated, new_weights)


def solution(mesh):
    return jax.shard_map(
        body,
        mesh=mesh,
        in_specs=(P("worker", "shard"), P("worker", "shard"), P("shard")),
        out_specs=(P("worker", "shard"), P("shard")),
        check_vma=False,
    )
```

profile of v0, /device:TPU:0, one launch (start us, length us, event | category | flops | bytes accessed | tf_op | source)
XLA Modules:
  0.0 88.2 jit_solution(14051908298596978391)
XLA Ops:
  7.2 5.7 %multiply_add_fusion = f32[1,524288]{1,0:T(1,128)} fusion(f32[1,524288]{1,0:T(1,128)} %param.6, f32[1,524288]{1,0:T(1,128)} %param.5), kind=kLoop, calls=%fused_computation.7 | loop fusion | flops 1048576 | bytes 6291456 | tf_op jit(solution)/shard_map/add | solution.py:29
  12.8 5.2 %all-to-all-start = ((f32[8,512,128]{2,1,0:T(8,128)}), f32[8,512,128]{2,1,0:T(8,128)S(1)}, u32[]{:S(2)}, u32[]{:S(2)}) async-start(f32[8,512,128]{2,1,0:T(8,128)} %bitcast.24), calls=%async_computation | async-start | bytes 4194304 | tf_op jit(solution)/shard_map/all_to_all | solution.py:35
  18.0 0.0 all-gather.2.cloned.1.call-start
  18.0 26.6 %all-to-all-done = f32[8,512,128]{2,1,0:T(8,128)S(1)} async-done(((f32[8,512,128]{2,1,0:T(8,128)}), f32[8,512,128]{2,1,0:T(8,128)S(1)}, u32[]{:S(2)}, u32[]{:S(2)}) %all-to-all-start) | async-done | bytes 2097184 | tf_op jit(solution)/shard_map/all_to_all | solution.py:35
  44.6 4.5 %while.10 = (s32[]{:T(128)}, f32[8,512,128]{2,1,0:T(8,128)S(1)}, s32[]{:T(128)}) while((s32[]{:T(128)}, f32[8,512,128]{2,1,0:T(8,128)S(1)}, s32[]{:T(128)}) %tuple.31), condition=%wide.region_1.0_spmd, body=%wide.region_0.0_spmd.sunk | while | flops 2883586 | bytes 30408748 | solution.py:23
  44.6 0.2 minimum_bitcast_fusion.4
  44.8 0.1 pad_maximum_fusion.6
  45.0 0.1 copy.12
  45.1 0.1 slice.52
  45.3 0.1 minimum_bitcast_fusion.5
  45.4 0.1 pad_maximum_fusion.7
  45.5 0.1 copy.13
  45.6 0.1 pad_maximum_fusion.8
  45.8 0.2 minimum_bitcast_fusion.4
  45.9 0.1 pad_maximum_fusion.6
  46.1 0.1 copy.12
  46.3 0.1 slice.52
  46.4 0.1 minimum_bitcast_fusion.5
  46.5 0.1 pad_maximum_fusion.7
  46.6 0.1 copy.13
  46.7 0.1 pad_maximum_fusion.8
  46.9 0.2 minimum_bitcast_fusion.4
  47.0 0.1 pad_maximum_fusion.6
  47.2 0.1 copy.12
  47.4 0.1 slice.52
  47.5 0.1 minimum_bitcast_fusion.5
  47.6 0.1 pad_maximum_fusion.7
  47.7 0.1 copy.13
  47.8 0.1 pad_maximum_fusion.8
  48.0 0.2 minimum_bitcast_fusion.4
  48.2 0.1 pad_maximum_fusion.6
  48.3 0.1 copy.12
  48.5 0.1 slice.52
  48.6 0.1 minimum_bitcast_fusion.5
  48.7 0.1 pad_maximum_fusion.7
  48.8 0.1 copy.13
  49.0 0.1 pad_maximum_fusion.8
  49.1 0.1 slice_reduce_fusion
  49.2 1.7 %bitcast_subtract_fusion = f32[65536]{0:T(1024)} fusion(f32[512,128]{1,0:T(8,128)S(1)} %slice_reduce_fusion, f32[524288]{0:T(1024)} %param.7, s32[]{:T(128)S(6)} %select_n.3), kind=kLoop, calls=%fused_computation.9 | loop fusion | flops 131072 | bytes 786436 | tf_op jit(solution)/shard_map/sub | solution.py:39
  50.9 0.0 all-gather.2.cloned.1.call-update
  50.9 27.5 %all-gather.2.cloned.1.call-done = f32[524288]{0:T(1024)} async-done(((f32[65536]{0:T(1024)}), f32[524288]{0:T(1024)}) %all-gather.2.cloned.1.call-update) | async-done | bytes 2097168 | tf_op jit(solution)/shard_map/all_gather | solution.py:40
  78.3 3.0 %copy.22 = f32[524288]{0:T(1024)} copy(f32[524288]{0:T(1024)} %all-gather.2.cloned.1.call-done) | data formatting | bytes 4194304
  (4 shorter events, 0.1 us)
Async XLA Ops:
  12.8 31.8 %all-to-all-start = ((f32[8,512,128]{2,1,0:T(8,128)}), f32[8,512,128]{2,1,0:T(8,128)S(1)}, u32[]{:S(2)}, u32[]{:S(2)}) async-start(f32[8,512,128]{2,1,0:T(8,128)} %bitcast.24), calls=%async_computation | async-start | bytes 4194304 | tf_op jit(solution)/shard_map/all_to_all | solution.py:35
  18.0 60.3 %all-gather.2.cloned.1.call-start = ((), (), s32[]{:S(2)}) async-start(), calls=%async_computation.1 | async-start | bytes 2359296 | tf_op jit(solution)/shard_map/all_gather | solution.py:40
Sparse Core Ops, SparseCore 0:
  51.0 27.2 all-gather.1
where the time goes:
time: 88.6 us; the launch traced here: 88.2 us
  waiting for transfers between devices  54.1 us (61%)
  between operations  14 us (16%)
  other arithmetic  10 us (11%)
  starting transfers between devices  5.21 us (6%)
  local copies, waits for them, and re-layouts  4.56 us (5%)
    all_gather x1, waiting for transfers between devices, body(): new_weights = lax.all_gather(own_new, 'worker', axis=0, tiled=True)  27.5 us
    all_to_all x1, waiting for transfers between devices, body(): lax.all_to_all(blocks, 'worker', split_axis=0, concat_axis=0, tiled=True)  26.6 us
    add x1, other arithmetic, body(): updated = 0.9 * momentum + gradient  5.66 us
    all_to_all x1, starting transfers between devices, body(): lax.all_to_all(blocks, 'worker', split_axis=0, concat_axis=0, tiled=True)  5.17 us
    unnamed x1, local copies, waits for them, and re-layouts  3.04 us
    another operation x16, other arithmetic, order_pairs(): jnp.stack([jnp.minimum(former, latter), jnp.maximum(former, latter)], 1)  2.06 us
  transfers between devices with their start and end apart: 2, of which 2 were waited for; matrix products, arithmetic and copies ran while one was open for 0% of the time, Pallas kernels for 0%

commit v1 on v0

v1 whole, which is shorter than its diff:
```python
import functools

import jax
import jax.numpy as jnp
from jax import lax
from jax.experimental import pallas as pl
from jax.experimental.pallas import tpu as pltpu
from jax.sharding import PartitionSpec as P

LANES = 128
CORES = 2
ANY = pl.BlockSpec(memory_space=pl.ANY)


def partner(worker, mask, count):
    if count & (count - 1) == 0:
        return worker ^ mask
    return (mask - worker) % count


def block_of(worker, count):
    chips = count // CORES
    return (worker % CORES) * chips + worker // CORES


def order_pair(values, low, high):
    former, latter = values[low], values[high]
    values[low] = jnp.minimum(former, latter)
    values[high] = jnp.maximum(former, latter)


def network(count):
    pairs = []
    span = 1
    while span < count:
        step = span
        while step >= 1:
            for first in range(step % span, count - step, 2 * step):
                for low in range(first, min(first + step, count - step)):
                    if low // (2 * span) == (low + step) // (2 * span):
                        pairs.append((low, low + step))
            step //= 2
        span *= 2
    return pairs


def kept_mean(values):
    values = list(values)
    count = len(values)
    trim = count // 4
    for low, high in network(count):
        order_pair(values, low, high)
    total = functools.reduce(jnp.add, values[trim : count - trim])
    return total / (count - 2 * trim)


def update_kernel(workers, masks, rows, m_ref, g_ref, u_ref, *rest):
    sends = rest[: len(masks)]
    m_buf, g_buf, in_sem, out_sem = rest[len(masks) :]
    me = lax.axis_index("worker")
    spans, loads = [], []
    for i, mask in enumerate(masks):
        start = pl.multiple_of(block_of(partner(me, mask, workers), workers) * rows, 8)
        span = pl.ds(start, rows)
        pair = [
            pltpu.make_async_copy(m_ref.at[span], m_buf.at[i], in_sem.at[2 * i]),
            pltpu.make_async_copy(g_ref.at[span], g_buf.at[i], in_sem.at[2 * i + 1]),
        ]
        for copy in pair:
            copy.start()
        spans.append(span)
        loads.append(pair)
    stores = []
    for i in range(len(masks)):
        for copy in loads[i]:
            copy.wait()
        g_buf[i] = 0.9 * m_buf[i] + g_buf[i]
        pair = [
            pltpu.make_async_copy(g_buf.at[i], sends[i], out_sem.at[2 * i]),
            pltpu.make_async_copy(g_buf.at[i], u_ref.at[spans[i]], out_sem.at[2 * i + 1]),
        ]
        for copy in pair:
            copy.start()
        stores += pair
    for copy in stores:
        copy.wait()


def update(momentum, gradient, workers, masks):
    rows = momentum.shape[0] // workers
    block = jax.ShapeDtypeStruct((rows, LANES), jnp.float32)
    out = pl.pallas_call(
        functools.partial(update_kernel, workers, masks, rows),
        out_shape=[jax.ShapeDtypeStruct(momentum.shape, jnp.float32)] + [block] * len(masks),
        in_specs=[ANY, ANY],
        out_specs=[ANY] + [ANY] * len(masks),
        scratch_shapes=[
            pltpu.VMEM((len(masks), rows, LANES), jnp.float32),
            pltpu.VMEM((len(masks), rows, LANES), jnp.float32),
            pltpu.SemaphoreType.DMA((2 * len(masks),)),
            pltpu.SemaphoreType.DMA((2 * len(masks),)),
        ],
        compiler_params=pltpu.CompilerParams(vmem_limit_bytes=16 << 20),
        name="update",
    )(momentum, gradient)
    return out[0], out[1:]


def trim_kernel(workers, rows, w_ref, *rest):
    blocks = rest[:workers]
    o_ref, w_buf, sem = rest[workers:]
    me = lax.axis_index("worker")
    start = pl.multiple_of(block_of(me, workers) * rows, 8)
    copy = pltpu.make_async_copy(w_ref.at[pl.ds(start, rows)], w_buf, sem)
    copy.start()
    copy.wait()
    step = 8 * max(1, 32 // workers)

    def one(i, carry):
        span = pl.ds(pl.multiple_of(i * step, step), step)
        mean = kept_mean([block[span] for block in blocks])
        o_ref[span] = w_buf[span] - 0.1 * mean
        return carry

    lax.fori_loop(0, rows // step, one, 0)


def trim(weights, blocks, workers):
    rows = blocks[0].shape[0]
    vmem = pl.BlockSpec(memory_space=pltpu.VMEM)
    return pl.pallas_call(
        functools.partial(trim_kernel, workers, rows),
        out_shape=jax.ShapeDtypeStruct((rows, LANES), jnp.float32),
        in_specs=[ANY] + [vmem] * workers,
        out_specs=vmem,
        scratch_shapes=[pltpu.VMEM((rows, LANES), jnp.float32), pltpu.SemaphoreType.DMA],
        compiler_params=pltpu.CompilerParams(vmem_limit_bytes=16 << 20),
        name="trim",
    )(weights, *blocks)


def place_kernel(workers, rows, *rest):
    blocks, o_ref, sem = rest[:workers], rest[workers], rest[workers + 1]
    me = lax.axis_index("worker")
    copies = []
    for mask, block in enumerate(blocks):
        start = pl.multiple_of(block_of(partner(me, mask, workers), workers) * rows, 8)
        copies.append(pltpu.make_async_copy(block, o_ref.at[pl.ds(start, rows)], sem.at[mask]))
        copies[-1].start()
    for copy in copies:
        copy.wait()


def place(blocks, workers):
    rows = blocks[0].shape[0]
    return pl.pallas_call(
        functools.partial(place_kernel, workers, rows),
        out_shape=jax.ShapeDtypeStruct((workers * rows, LANES), jnp.float32),
        in_specs=[ANY] * workers,
        out_specs=ANY,
        scratch_shapes=[pltpu.SemaphoreType.DMA((workers,))],
        compiler_params=pltpu.CompilerParams(vmem_limit_bytes=16 << 20),
        name="place",
    )(*blocks)


def hbm(x):
    return pltpu.with_memory_space_constraint(x, pltpu.HBM)


def body(momentum, gradient, weights):
    workers = lax.axis_size("worker")

    def swap(block, mask):
        pairs = [(w, partner(w, mask, workers)) for w in range(workers)]
        return lax.ppermute(block, "worker", pairs)

    masks = list(range(workers))
    updated, sends = update(
        hbm(momentum.reshape(-1, LANES)), hbm(gradient.reshape(-1, LANES)), workers, masks
    )
    blocks = [sends[m] if m == 0 else swap(sends[m], m) for m in masks]
    own = trim(hbm(weights.reshape(-1, LANES)), blocks, workers)
    mine = {m: own if m == 0 else swap(own, m) for m in range(0, workers, CORES)}
    theirs = {m + 1: swap(mine[m], 1) for m in mine}
    new_weights = place([(mine | theirs)[m] for m in masks], workers)
    return updated.reshape(momentum.shape), new_weights.reshape(weights.shape)


def solution(mesh):
    return jax.shard_map(
        body,
        mesh=mesh,
        in_specs=(P("worker", "shard"), P("worker", "shard"), P("shard")),
        out_specs=(P("worker", "shard"), P("shard")),
        check_vma=False,
    )
```

time: 88.6 us -> 52.2 us (0.59)
  waiting for transfers between devices: 54.1 us -> 32.1 us
  between operations: 14 us -> 0.66 us
  other arithmetic: 10 us -> 0 us
  starting transfers between devices: 5.21 us -> 13.1 us
  Pallas kernels: 0 us -> 6.29 us
  local copies, waits for them, and re-layouts: 4.56 us -> 0 us
    ppermute x0 -> x14, waiting for transfers between devices: none -> 32.1 us  [swap(): return lax.ppermute(block, 'worker', pairs)]
    all_gather x1 -> x0, waiting for transfers between devices: 27.5 us -> none  [body(): new_weights = lax.all_gather(own_new, 'worker', axis=0, tiled=True)]
    all_to_all x1 -> x0, waiting for transfers between devices: 26.6 us -> none  [body(): lax.all_to_all(blocks, 'worker', split_axis=0, concat_axis=0, tiled=True)]
    ppermute x0 -> x14, starting transfers between devices: none -> 13.1 us  [swap(): return lax.ppermute(block, 'worker', pairs)]
    pallas_call x0 -> x3, Pallas kernels: none -> 6.29 us  [the longest x1 3.46 us: update(): pl.pallas_call(functools.partial(update_kernel, workers, masks, rows), ou...]
    add x1 -> x0, other arithmetic: 5.66 us -> none  [body(): updated = 0.9 * momentum + gradient]
    all_to_all x1 -> x0, starting transfers between devices: 5.17 us -> none  [body(): lax.all_to_all(blocks, 'worker', split_axis=0, concat_axis=0, tiled=True)]
    unnamed x1 -> x0, local copies, waits for them, and re-layouts: 3.04 us -> none
  transfers between devices with their start and end apart: 2 -> 14, of which waited for: 2 -> 8; matrix products, arithmetic and copies ran while one was open for 0% -> 0% of each run, Pallas kernels for 0% -> 0%
where the time goes in v1:
time: 52.2 us; the launch traced here: 52.1 us
  waiting for transfers between devices  32.1 us (61%)
  starting transfers between devices  13.1 us (25%)
  Pallas kernels  6.29 us (12%)
  between operations  0.66 us (1%)
    ppermute x14, waiting for transfers between devices, swap(): return lax.ppermute(block, 'worker', pairs)  32.1 us
    ppermute x14, starting transfers between devices, swap(): return lax.ppermute(block, 'worker', pairs)  13.1 us
    pallas_call x1, Pallas kernels, update(): pl.pallas_call(functools.partial(update_kernel, workers, masks, rows), ou...  3.46 us
    pallas_call x1, Pallas kernels, trim(): pl.pallas_call(functools.partial(trim_kernel, workers, rows), out_shape=j...  1.46 us
    pallas_call x1, Pallas kernels, place(): pl.pallas_call(functools.partial(place_kernel, workers, rows), out_shape=...  1.37 us
  transfers between devices with their start and end apart: 14, of which 8 were waited for; matrix products, arithmetic and copies ran while one was open for 0% of the time, Pallas kernels for 0%

profile of v1, /device:TPU:0, one launch (start us, length us, event | category | flops | bytes accessed | tf_op | source)
XLA Modules:
  0.0 52.1 jit_solution(5853436833358333088)
XLA Ops:
  0.6 3.5 %update.1 = (f32[4096,128]{1,0:T(8,128)}, f32[512,128]{1,0:T(8,128)S(1)}, f32[512,128]{1,0:T(8,128)S(1)}, f32[512,128]{1,0:T(8,128)S(1)}, f32[512,128]{1,0:T(8,1...) custom-call(f32[4096,128]{1,0:T(8,128)} %bitcast.5, ...), custom_call_target="tpu_custom_call" | custom-call | tf_op jit(solution)/shard_map/update/pallas_call | solution.py:92
  4.1 0.5 collective-permute-start
  4.6 2.6 %collective-permute-start.1 = (f32[512,128]{1,0:T(8,128)S(1)}, f32[512,128]{1,0:T(8,128)S(1)}, u32[]{:S(2)}, u32[]{:S(2)}) collective-permute-start(f32[512,128]{1,0:T(8,128)S(1)} %get-tuple-element.14), channel_id=1, source_target_pairs={{0,8},{4,12},{8,0},{12,4},{16,24},{20,28},{24,16},{28,20},{1,9},{5... | collective-permute-start | bytes 786440 | tf_op jit(solution)/shard_map/ppermute | solution.py:176
  7.2 0.1 collective-permute-start.2
  7.2 1.8 %collective-permute-start.3 = (f32[512,128]{1,0:T(8,128)S(1)}, f32[512,128]{1,0:T(8,128)S(1)}, u32[]{:S(2)}, u32[]{:S(2)}) collective-permute-start(f32[512,128]{1,0:T(8,128)S(1)} %get-tuple-element.16), channel_id=1, source_target_pairs={{0,16},{4,20},{8,24},{12,28},{16,0},{20,4},{24,8},{28,12},{1,17},{... | collective-permute-start | bytes 786440 | tf_op jit(solution)/shard_map/ppermute | solution.py:176
  9.0 0.0 collective-permute-start.4
  9.0 0.0 collective-permute-done.rest_1_
  9.0 2.6 %collective-permute-start.5 = (f32[512,128]{1,0:T(8,128)S(1)}, f32[512,128]{1,0:T(8,128)S(1)}, u32[]{:S(2)}, u32[]{:S(2)}) collective-permute-start(f32[512,128]{1,0:T(8,128)S(1)} %get-tuple-element.18), channel_id=1, source_target_pairs={{0,24},{4,28},{8,16},{12,20},{16,8},{20,12},{24,0},{28,4},{1,25},{... | collective-permute-start | bytes 786440 | tf_op jit(solution)/shard_map/ppermute | solution.py:176
  11.6 2.7 %collective-permute-done.1.rest_2_ = f32[512,128]{1,0:T(8,128)S(1)} collective-permute-done((f32[512,128]{1,0:T(8,128)S(1)}, f32[512,128]{1,0:T(8,128)S(1)}, u32[]{:S(2)}, u32[]{:S(2)}) %collective-permute-start.1) | collective-permute-done | bytes 262176 | tf_op jit(solution)/shard_map/ppermute | solution.py:176
  14.3 1.7 %collective-permute-start.6 = (f32[512,128]{1,0:T(8,128)S(1)}, f32[512,128]{1,0:T(8,128)S(1)}, u32[]{:S(2)}, u32[]{:S(2)}) collective-permute-start(f32[512,128]{1,0:T(8,128)S(1)} %get-tuple-element.19), channel_id=1, source_target_pairs={{0,28},{4,24},{8,20},{12,16},{16,12},{20,8},{24,4},{28,0},{1,29},{... | collective-permute-start | bytes 786440 | tf_op jit(solution)/shard_map/ppermute | solution.py:176
  16.1 3.4 %collective-permute-done.2.rest_3_ = f32[512,128]{1,0:T(8,128)S(1)} collective-permute-done((f32[512,128]{1,0:T(8,128)S(1)}, f32[512,128]{1,0:T(8,128)S(1)}, u32[]{:S(2)}, u32[]{:S(2)}) %collective-permute-start.2) | collective-permute-done | bytes 262176 | tf_op jit(solution)/shard_map/ppermute | solution.py:176
  19.4 0.0 collective-permute-done.3.rest_4_
  19.4 12.5 %collective-permute-done.4.rest_5_ = f32[512,128]{1,0:T(8,128)S(1)} collective-permute-done((f32[512,128]{1,0:T(8,128)S(1)}, f32[512,128]{1,0:T(8,128)S(1)}, u32[]{:S(2)}, u32[]{:S(2)}) %collective-permute-start.4) | collective-permute-done | bytes 262176 | tf_op jit(solution)/shard_map/ppermute | solution.py:176
  31.9 0.0 collective-permute-done.5.rest_6_
  31.9 0.0 collective-permute-done.6.rest_7_
  31.9 1.5 %trim.1.rest_0_ = f32[512,128]{1,0:T(8,128)S(1)} custom-call(f32[4096,128]{1,0:T(8,128)} %bitcast.7, f32[512,128]{1,0:T(8,128)S(1)} %get-tuple-element.12.rest_0_, f32[512,128]{1,0:T(8,128)S(1)} %collective-permute-done.rest_1_, f32[512,128]{1,0:T(8,128)S(1)} %collective-permute-done.1.rest_2_, f32[512,128]{1,0:T(8,128)S(1)} %collective-permute-done.2.rest_3_, ...), custom_call_target="tpu_custom_call" | custom-call | tf_op jit(solution)/shard_map/trim/pallas_call | solution.py:131
  33.4 2.9 %collective-permute-start.12 = (f32[512,128]{1,0:T(8,128)S(1)}, f32[512,128]{1,0:T(8,128)S(1)}, u32[]{:S(2)}, u32[]{:S(2)}) collective-permute-start(f32[512,128]{1,0:T(8,128)S(1)} %trim.1.rest_0_), channel_id=1, source_target_pairs={{0,24},{4,28},{8,16},{12,20},{16,8},{20,12},{24,0},{28,4},{1,25},{... | collective-permute-start | bytes 786440 | tf_op jit(solution)/shard_map/ppermute | solution.py:176
  36.3 0.5 collective-permute-start.10
  36.8 0.1 collective-permute-start.8
  37.0 0.0 collective-permute-start.7
  37.0 6.5 %collective-permute-done.12.rest_6_ = f32[512,128]{1,0:T(8,128)S(1)} collective-permute-done((f32[512,128]{1,0:T(8,128)S(1)}, f32[512,128]{1,0:T(8,128)S(1)}, u32[]{:S(2)}, u32[]{:S(2)}) %collective-permute-start.12) | collective-permute-done | bytes 262176 | tf_op jit(solution)/shard_map/ppermute | solution.py:176
  43.5 0.0 collective-permute-start.13
  43.5 5.3 %collective-permute-done.10.rest_4_ = f32[512,128]{1,0:T(8,128)S(1)} collective-permute-done((f32[512,128]{1,0:T(8,128)S(1)}, f32[512,128]{1,0:T(8,128)S(1)}, u32[]{:S(2)}, u32[]{:S(2)}) %collective-permute-start.10) | collective-permute-done | bytes 262176 | tf_op jit(solution)/shard_map/ppermute | solution.py:176
  48.8 0.0 collective-permute-start.11
  48.8 0.3 collective-permute-done.8.rest_2_
  49.1 0.2 collective-permute-start.9
  49.3 0.0 collective-permute-done.7.rest_1_
  49.3 0.0 collective-permute-done.13.rest_7_
  49.3 1.0 %collective-permute-done.11.rest_5_ = f32[512,128]{1,0:T(8,128)S(1)} collective-permute-done((f32[512,128]{1,0:T(8,128)S(1)}, f32[512,128]{1,0:T(8,128)S(1)}, u32[]{:S(2)}, u32[]{:S(2)}) %collective-permute-start.11) | collective-permute-done | bytes 262176 | tf_op jit(solution)/shard_map/ppermute | solution.py:176
  50.3 0.4 collective-permute-done.9.rest_3_
  50.7 1.4 %place.1 = f32[4096,128]{1,0:T(8,128)} custom-call(f32[512,128]{1,0:T(8,128)S(1)} %trim.1.rest_0_, f32[512,128]{1,0:T(8,128)S(1)} %collective-permute-done.7.rest_1_, f32[512,128]{1,0:T(8,128)S(1)} %collective-permute-done.8.rest_2_, f32[512,128]{1,0:T(8,128)S(1)} %collective-permute-done.9.rest_3_, f32[512,128]{1,0:T(8,128)S(1)} %collective-permute-done.10.rest_4_, ...), custom_call_target="tpu_custom_call" | custom-call | tf_op jit(solution)/shard_map/place/pallas_call | solution.py:156
Async XLA Ops:
  4.1 4.9 %collective-permute-start = (f32[512,128]{1,0:T(8,128)S(1)}, f32[512,128]{1,0:T(8,128)S(1)}, u32[]{:S(2)}, u32[]{:S(2)}) collective-permute-start(f32[512,128]{1,0:T(8,128)S(1)} %get-tuple-element.13), channel_id=1, source_target_pairs={{0,4},{4,0},{8,12},{12,8},{16,20},{20,16},{24,28},{28,24},{1,5},{5... | collective-permute-start | bytes 786440 | tf_op jit(solution)/shard_map/ppermute | solution.py:176
  4.6 9.7 %collective-permute-start.1 = (f32[512,128]{1,0:T(8,128)S(1)}, f32[512,128]{1,0:T(8,128)S(1)}, u32[]{:S(2)}, u32[]{:S(2)}) collective-permute-start(f32[512,128]{1,0:T(8,128)S(1)} %get-tuple-element.14), channel_id=1, source_target_pairs={{0,8},{4,12},{8,0},{12,4},{16,24},{20,28},{24,16},{28,20},{1,9},{5... | collective-permute-start | bytes 786440 | tf_op jit(solution)/shard_map/ppermute | solution.py:176
  7.2 12.3 %collective-permute-start.2 = (f32[512,128]{1,0:T(8,128)S(1)}, f32[512,128]{1,0:T(8,128)S(1)}, u32[]{:S(2)}, u32[]{:S(2)}) collective-permute-start(f32[512,128]{1,0:T(8,128)S(1)} %get-tuple-element.15), channel_id=1, source_target_pairs={{0,12},{4,8},{8,4},{12,0},{16,28},{20,24},{24,20},{28,16},{1,13},{... | collective-permute-start | bytes 786440 | tf_op jit(solution)/shard_map/ppermute | solution.py:176
  7.2 12.2 %collective-permute-start.3 = (f32[512,128]{1,0:T(8,128)S(1)}, f32[512,128]{1,0:T(8,128)S(1)}, u32[]{:S(2)}, u32[]{:S(2)}) collective-permute-start(f32[512,128]{1,0:T(8,128)S(1)} %get-tuple-element.16), channel_id=1, source_target_pairs={{0,16},{4,20},{8,24},{12,28},{16,0},{20,4},{24,8},{28,12},{1,17},{... | collective-permute-start | bytes 786440 | tf_op jit(solution)/shard_map/ppermute | solution.py:176
  9.0 22.9 %collective-permute-start.4 = (f32[512,128]{1,0:T(8,128)S(1)}, f32[512,128]{1,0:T(8,128)S(1)}, u32[]{:S(2)}, u32[]{:S(2)}) collective-permute-start(f32[512,128]{1,0:T(8,128)S(1)} %get-tuple-element.17), channel_id=1, source_target_pairs={{0,20},{4,16},{8,28},{12,24},{16,4},{20,0},{24,12},{28,8},{1,21},{... | collective-permute-start | bytes 786440 | tf_op jit(solution)/shard_map/ppermute | solution.py:176
  9.0 22.9 %collective-permute-start.5 = (f32[512,128]{1,0:T(8,128)S(1)}, f32[512,128]{1,0:T(8,128)S(1)}, u32[]{:S(2)}, u32[]{:S(2)}) collective-permute-start(f32[512,128]{1,0:T(8,128)S(1)} %get-tuple-element.18), channel_id=1, source_target_pairs={{0,24},{4,28},{8,16},{12,20},{16,8},{20,12},{24,0},{28,4},{1,25},{... | collective-permute-start | bytes 786440 | tf_op jit(solution)/shard_map/ppermute | solution.py:176
  14.3 17.6 %collective-permute-start.6 = (f32[512,128]{1,0:T(8,128)S(1)}, f32[512,128]{1,0:T(8,128)S(1)}, u32[]{:S(2)}, u32[]{:S(2)}) collective-permute-start(f32[512,128]{1,0:T(8,128)S(1)} %get-tuple-element.19), channel_id=1, source_target_pairs={{0,28},{4,24},{8,20},{12,16},{16,12},{20,8},{24,4},{28,0},{1,29},{... | collective-permute-start | bytes 786440 | tf_op jit(solution)/shard_map/ppermute | solution.py:176
  33.4 10.1 %collective-permute-start.12 = (f32[512,128]{1,0:T(8,128)S(1)}, f32[512,128]{1,0:T(8,128)S(1)}, u32[]{:S(2)}, u32[]{:S(2)}) collective-permute-start(f32[512,128]{1,0:T(8,128)S(1)} %trim.1.rest_0_), channel_id=1, source_target_pairs={{0,24},{4,28},{8,16},{12,20},{16,8},{20,12},{24,0},{28,4},{1,25},{... | collective-permute-start | bytes 786440 | tf_op jit(solution)/shard_map/ppermute | solution.py:176
  36.3 12.4 %collective-permute-start.10 = (f32[512,128]{1,0:T(8,128)S(1)}, f32[512,128]{1,0:T(8,128)S(1)}, u32[]{:S(2)}, u32[]{:S(2)}) collective-permute-start(f32[512,128]{1,0:T(8,128)S(1)} %trim.1.rest_0_), channel_id=1, source_target_pairs={{0,16},{4,20},{8,24},{12,28},{16,0},{20,4},{24,8},{28,12},{1,17},{... | collective-permute-start | bytes 786440 | tf_op jit(solution)/shard_map/ppermute | solution.py:176
  36.8 12.3 %collective-permute-start.8 = (f32[512,128]{1,0:T(8,128)S(1)}, f32[512,128]{1,0:T(8,128)S(1)}, u32[]{:S(2)}, u32[]{:S(2)}) collective-permute-start(f32[512,128]{1,0:T(8,128)S(1)} %trim.1.rest_0_), channel_id=1, source_target_pairs={{0,8},{4,12},{8,0},{12,4},{16,24},{20,28},{24,16},{28,20},{1,9},{5... | collective-permute-start | bytes 786440 | tf_op jit(solution)/shard_map/ppermute | solution.py:176
  37.0 12.3 %collective-permute-start.7 = (f32[512,128]{1,0:T(8,128)S(1)}, f32[512,128]{1,0:T(8,128)S(1)}, u32[]{:S(2)}, u32[]{:S(2)}) collective-permute-start(f32[512,128]{1,0:T(8,128)S(1)} %trim.1.rest_0_), channel_id=1, source_target_pairs={{0,4},{4,0},{8,12},{12,8},{16,20},{20,16},{24,28},{28,24},{1,5},{5... | collective-permute-start | bytes 786440 | tf_op jit(solution)/shard_map/ppermute | solution.py:176
  43.5 5.8 %collective-permute-start.13 = (f32[512,128]{1,0:T(8,128)S(1)}, f32[512,128]{1,0:T(8,128)S(1)}, u32[]{:S(2)}, u32[]{:S(2)}) collective-permute-start(f32[512,128]{1,0:T(8,128)S(1)} %collective-permute-done.12.rest_6_), channel_id=1, source_target_pairs={{0,4},{4,0},{8,12},{12,8},{16,20},{20,16},{24,28},{28,24},{1,5},{5... | collective-permute-start | bytes 786440 | tf_op jit(solution)/shard_map/ppermute | solution.py:176
  48.8 1.5 %collective-permute-start.11 = (f32[512,128]{1,0:T(8,128)S(1)}, f32[512,128]{1,0:T(8,128)S(1)}, u32[]{:S(2)}, u32[]{:S(2)}) collective-permute-start(f32[512,128]{1,0:T(8,128)S(1)} %collective-permute-done.10.rest_4_), channel_id=1, source_target_pairs={{0,4},{4,0},{8,12},{12,8},{16,20},{20,16},{24,28},{28,24},{1,5},{5... | collective-permute-start | bytes 786440 | tf_op jit(solution)/shard_map/ppermute | solution.py:176
  49.1 1.6 %collective-permute-start.9 = (f32[512,128]{1,0:T(8,128)S(1)}, f32[512,128]{1,0:T(8,128)S(1)}, u32[]{:S(2)}, u32[]{:S(2)}) collective-permute-start(f32[512,128]{1,0:T(8,128)S(1)} %collective-permute-done.8.rest_2_), channel_id=1, source_target_pairs={{0,4},{4,0},{8,12},{12,8},{16,20},{20,16},{24,28},{28,24},{1,5},{5... | collective-permute-start | bytes 786440 | tf_op jit(solution)/shard_map/ppermute | solution.py:176

commit v2 on v1

v2 whole, which is shorter than its diff:
```python
import functools

import jax
import jax.numpy as jnp
from jax import lax
from jax.experimental import pallas as pl
from jax.experimental.pallas import tpu as pltpu
from jax.sharding import PartitionSpec as P

LANES = 128
DEPTH = 4
LATER = 2
CORES = 2


def cost(size):
    return pl.CostEstimate(flops=size, bytes_accessed=4 * size, transcendentals=0)


ANY = pl.BlockSpec(memory_space=pl.ANY)
VMEM = pl.BlockSpec(memory_space=pltpu.VMEM)


def turned(label, core, chips):
    bits = chips.bit_length() - 1
    second = sum(1 << (j + 1) % bits for j in range(bits) if label >> j & 1) if bits else 0
    return label + core * (second - label)


def other_chip(chip, label, core, chips):
    if chips & (chips - 1) == 0:
        return chip ^ turned(label, core, chips)
    return (label - chip) % chips


def target(worker, label, flip, count):
    chip, core = worker // CORES, worker % CORES
    core_there = core + flip * (1 - 2 * core)
    return CORES * other_chip(chip, label, core, count // CORES) + core_there


def origin(worker, label, flip, count):
    chip, core = worker // CORES, worker % CORES
    core_there = core + flip * (1 - 2 * core)
    return CORES * other_chip(chip, label, core_there, count // CORES) + core_there


def block_of(worker, count):
    chips = count // CORES
    return (worker % CORES) * chips + worker // CORES


def order_pair(values, low, high):
    former, latter = values[low], values[high]
    values[low] = jnp.minimum(former, latter)
    values[high] = jnp.maximum(former, latter)


def network(count):
    pairs = []
    span = 1
    while span < count:
        step = span
        while step >= 1:
            for first in range(step % span, count - step, 2 * step):
                for low in range(first, min(first + step, count - step)):
                    if low // (2 * span) == (low + step) // (2 * span):
                        pairs.append((low, low + step))
            step //= 2
        span *= 2
    return pairs


def kept_mean(values):
    values = list(values)
    count = len(values)
    trim = count // 4
    for low, high in network(count):
        order_pair(values, low, high)
    total = functools.reduce(jnp.add, values[trim : count - trim])
    return total / (count - 2 * trim)


def send_kernel(workers, routes, cuts, rows, deps, m_ref, g_ref, *rest):
    rest = rest[deps:]
    count = sum(len(cut) - 1 for cut in cuts)
    sends = rest[:count]
    m_buf, g_buf, sem = rest[count:]
    me = lax.axis_index("worker")
    loads = []
    for i, route in enumerate(routes):
        start = pl.multiple_of(block_of(target(me, *route, workers), workers) * rows, 8)
        span = pl.ds(start, rows)
        pair = [
            pltpu.make_async_copy(m_ref.at[span], m_buf.at[i], sem.at[2 * i]),
            pltpu.make_async_copy(g_ref.at[span], g_buf.at[i], sem.at[2 * i + 1]),
        ]
        for copy in pair:
            copy.start()
        loads.append(pair)
    at = 0
    for i, cut in enumerate(cuts):
        for copy in loads[i]:
            copy.wait()
        for low, high in zip(cut[:-1], cut[1:]):
            sends[at][...] = 0.9 * m_buf[i, low:high] + g_buf[i, low:high]
            at += 1


def send_blocks(momentum, gradient, workers, routes, cuts, deps, name):
    rows = momentum.shape[0] // workers
    sizes = [high - low for cut in cuts for low, high in zip(cut[:-1], cut[1:])]
    return pl.pallas_call(
        functools.partial(send_kernel, workers, routes, cuts, rows, len(deps)),
        out_shape=[jax.ShapeDtypeStruct((size, LANES), jnp.float32) for size in sizes],
        in_specs=[ANY] * (2 + len(deps)),
        out_specs=[VMEM] * len(sizes),
        scratch_shapes=[
            pltpu.VMEM((len(routes), rows, LANES), jnp.float32),
            pltpu.VMEM((len(routes), rows, LANES), jnp.float32),
            pltpu.SemaphoreType.DMA((2 * len(routes),)),
        ],
        compiler_params=pltpu.CompilerParams(vmem_limit_bytes=16 << 20),
        cost_estimate=cost(3 * LANES * sum(sizes)),
        name=name,
    )(momentum, gradient, *deps)


def update_kernel(workers, pieces, rows, deps, m_ref, g_ref, w_ref, *rest):
    u_ref, own_ref, m_buf, g_buf, in_sem, out_sem, own_sem = rest[deps:]
    size = own_ref.shape[0]
    start = pl.multiple_of(block_of(lax.axis_index("worker"), workers) * size, 8)
    loads, stores = [], []
    for i in range(pieces):
        span = pl.ds(i * rows, rows)
        loads.append(
            [
                pltpu.make_async_copy(m_ref.at[span], m_buf.at[i], in_sem.at[2 * i]),
                pltpu.make_async_copy(g_ref.at[span], g_buf.at[i], in_sem.at[2 * i + 1]),
            ]
        )
        stores.append(pltpu.make_async_copy(g_buf.at[i], u_ref.at[span], out_sem.at[i]))
        for copy in loads[i]:
            copy.start()
    own = pltpu.make_async_copy(w_ref.at[pl.ds(start, size)], own_ref, own_sem)
    own.start()
    for i in range(pieces):
        for copy in loads[i]:
            copy.wait()
        g_buf[i] = 0.9 * m_buf[i] + g_buf[i]
        stores[i].start()
    for copy in stores + [own]:
        copy.wait()


def update(momentum, gradient, weights, workers, pieces, deps):
    rows = momentum.shape[0] // pieces
    own = (weights.shape[0] // workers, LANES)
    return pl.pallas_call(
        functools.partial(update_kernel, workers, pieces, rows, len(deps)),
        out_shape=[
            jax.ShapeDtypeStruct(momentum.shape, jnp.float32),
            jax.ShapeDtypeStruct(own, jnp.float32),
        ],
        in_specs=[ANY] * (3 + len(deps)),
        out_specs=[ANY, VMEM],
        scratch_shapes=[
            pltpu.VMEM((pieces, rows, LANES), jnp.float32),
            pltpu.VMEM((pieces, rows, LANES), jnp.float32),
            pltpu.SemaphoreType.DMA((2 * pieces,)),
            pltpu.SemaphoreType.DMA((pieces,)),
            pltpu.SemaphoreType.DMA,
        ],
        compiler_params=pltpu.CompilerParams(vmem_limit_bytes=16 << 20),
        cost_estimate=cost(3 * momentum.size),
        name="update",
    )(momentum, gradient, weights, *deps)


def trim_kernel(size, starts, *rest):
    blocks, o_ref = rest[: len(starts)], rest[-1]
    step = 8 * max(1, 32 // (len(starts) - 1))

    def one(i, carry):
        at = pl.multiple_of(i * step, step)
        own, *values = [b[pl.ds(s + at, step)] for b, s in zip(blocks, starts)]
        o_ref[pl.ds(at, step)] = own - 0.1 * kept_mean(values)
        return carry

    lax.fori_loop(0, size // step, one, 0)


def trim(weights, blocks, low, high, deps, name):
    rows = weights.shape[0]
    size = high - low
    starts = [low if block.shape[0] == rows else 0 for block in [weights, *blocks]]
    return pl.pallas_call(
        functools.partial(trim_kernel, size, starts),
        out_shape=jax.ShapeDtypeStruct((size, LANES), jnp.float32),
        in_specs=[VMEM] * len(starts) + [ANY] * len(deps),
        out_specs=VMEM,
        compiler_params=pltpu.CompilerParams(vmem_limit_bytes=16 << 20),
        cost_estimate=cost((len(starts) + 1) * size * LANES),
        name=name,
    )(weights, *blocks, *deps)


def place_kernel(workers, rows, places, *rest):
    blocks, (o_ref, sem) = rest[: len(places)], rest[len(places) :]
    me = lax.axis_index("worker")
    copies = []
    for i, (block, (low, *route)) in enumerate(zip(blocks, places)):
        start = block_of(origin(me, *route, workers), workers) * rows + low
        there = o_ref.at[pl.ds(pl.multiple_of(start, 8), block.shape[0])]
        copies.append(pltpu.make_async_copy(block, there, sem.at[i]))
        copies[i].start()
    for copy in copies:
        copy.wait()


def place(blocks, workers, rows):
    return pl.pallas_call(
        functools.partial(place_kernel, workers, rows, list(blocks)),
        out_shape=jax.ShapeDtypeStruct((workers * rows, LANES), jnp.float32),
        in_specs=[ANY] * len(blocks),
        out_specs=ANY,
        scratch_shapes=[pltpu.SemaphoreType.DMA((len(blocks),))],
        compiler_params=pltpu.CompilerParams(vmem_limit_bytes=16 << 20),
        cost_estimate=cost(2 * LANES * workers * rows),
        name="place",
    )(*blocks.values())


def copy_kernel(from_ref, *rest):
    rest[-1][...] = from_ref[...]


def copied(block, deps):
    return pl.pallas_call(
        copy_kernel,
        out_shape=jax.ShapeDtypeStruct(block.shape, jnp.float32),
        in_specs=[VMEM] + [ANY] * len(deps),
        out_specs=VMEM,
        compiler_params=pltpu.CompilerParams(vmem_limit_bytes=16 << 20),
        cost_estimate=cost(2 * block.size),
        name="copied",
    )(block, *deps)


def gate_kernel(*refs):
    del refs


def gate(blocks, deps):
    return pl.pallas_call(
        gate_kernel,
        out_shape=[jax.ShapeDtypeStruct(b.shape, b.dtype) for b in blocks],
        in_specs=[ANY] * (len(blocks) + len(deps)),
        out_specs=[ANY] * len(blocks),
        input_output_aliases={i: i for i in range(len(blocks))},
        compiler_params=pltpu.CompilerParams(vmem_limit_bytes=1 << 20),
        name="gate",
    )(*blocks, *deps)


def in_hbm(array):
    return pltpu.with_memory_space_constraint(array.reshape(-1, LANES), pltpu.HBM)


def body(momentum, gradient, weights):
    workers = lax.axis_size("worker")
    chips = workers // CORES
    m, g, w = in_hbm(momentum), in_hbm(gradient), in_hbm(weights)
    rows = m.shape[0] // workers
    cut = [0, rows // 2, rows]
    parts = list(zip(cut[:-1], cut[1:]))
    queue = []

    def send(block, route, deps=()):
        if deps:
            (block,) = gate([block], list(deps))
        pairs = [(i, target(i, *route, workers)) for i in range(workers)]
        return lax.ppermute(block, "worker", pairs)

    def queued(block, route, *deps):
        before = queue[-DEPTH : len(queue) - DEPTH + 1] if len(queue) >= DEPTH else []
        queue.append(send(block, route, [*deps, *before]))
        return queue[-1]

    far_chips = list(range(chips - 1, 0, -1))
    near_routes = [(label, 0) for label in far_chips]
    far_routes = [(label, 1) for label in far_chips]
    near = send_blocks(m, g, workers, near_routes, [[0, rows]] * len(near_routes), [], "near")
    held = [queued(block, route) for route, block in zip(near_routes, near)]
    routes = far_routes + [(0, 1), (0, 0)]
    cuts = [cut] * len(far_routes) + [[0, rows]] * 2
    sends = send_blocks(m, g, workers, routes, cuts, near[:1], "far")
    held += [send(sends[-2], (0, 1)), sends[-1]]
    updated, own_w = update(m, g, w, workers, workers, sends[:1])
    got = [[], []]
    for part in range(2):
        for i, route in enumerate(far_routes):
            early = part == 0 and i < DEPTH - len(near_routes)
            got[part].append(queued(sends[2 * i + part], route, *([] if early else [own_w])))

    gathered = []
    for got, (low, high) in zip(got, parts):
        new = [trim(own_w, held + got, low, high, [], "trim")]
        for label in range(1, chips):
            step = 1 << label.bit_length() - 1
            if chips & (chips - 1) == 0:
                new.append(send(new[label - step], (step, 0)))
            else:
                new.append(send(new[0], (label, 0)))
        gathered.append(new)
    blocks = {}
    for new, (low, high) in zip(gathered, parts):
        for label, block in enumerate(new):
            blocks[low, label, 0] = block
            if low == 0:
                block = copied(block, [gathered[1][min(LATER, chips - 1)]])
            blocks[low, label, 1] = send(block, (0, 1))
    result = place(blocks, workers, rows)
    return updated.reshape(momentum.shape), result.reshape(weights.shape)


def solution(mesh):
    return jax.shard_map(
        body,
        mesh=mesh,
        in_specs=(P("worker", "shard"), P("worker", "shard"), P("shard")),
        out_specs=(P("worker", "shard"), P("shard")),
        check_vma=False,
    )
```

time: 52.2 us -> 45.8 us (0.88)
  waiting for transfers between devices: 32.1 us -> 15 us
  starting transfers between devices: 13.1 us -> 21.3 us
  Pallas kernels: 6.29 us -> 8.58 us
    ppermute x14 -> x24, waiting for transfers between devices: 32.1 us -> 15 us  [send(): return lax.ppermute(block, 'worker', pairs)]
    ppermute x14 -> x24, starting transfers between devices: 13.1 us -> 21.3 us  [send(): return lax.ppermute(block, 'worker', pairs)]
    pallas_call x3 -> x15, Pallas kernels: 6.29 us -> 8.58 us  [the longest x1 3.37 us: update(): pl.pallas_call(functools.partial(update_kernel, workers, pieces, rows, le...]
  transfers between devices with their start and end apart: 14 -> 24, of which waited for: 8 -> 12; matrix products, arithmetic and copies ran while one was open for 0% -> 0% of each run, Pallas kernels for 0% -> 12%
where the time goes in v2:
time: 45.8 us; the launch traced here: 45.7 us
  starting transfers between devices  21.3 us (47%)
  waiting for transfers between devices  15 us (33%)
  Pallas kernels  8.58 us (19%)
  between operations  0.74 us (2%)
    ppermute x24, starting transfers between devices, send(): return lax.ppermute(block, 'worker', pairs)  21.3 us
    ppermute x24, waiting for transfers between devices, send(): return lax.ppermute(block, 'worker', pairs)  15 us
    pallas_call x1, Pallas kernels, update(): pl.pallas_call(functools.partial(update_kernel, workers, pieces, rows, le...  3.37 us
    pallas_call x2, Pallas kernels, send_blocks(): pl.pallas_call(functools.partial(send_kernel, workers, routes, cuts, rows...  3.23 us
    pallas_call x1, Pallas kernels, place(): pl.pallas_call(functools.partial(place_kernel, workers, rows, list(blocks...  1.44 us
  transfers between devices with their start and end apart: 24, of which 12 were waited for; matrix products, arithmetic and copies ran while one was open for 0% of the time, Pallas kernels for 12%

profile of v2, /device:TPU:0, one launch (start us, length us, event | category | flops | bytes accessed | tf_op | source)
XLA Modules:
  0.0 45.7 jit_solution(15988082896818728506)
XLA Ops:
  0.6 1.5 %near.1 = (f32[512,128]{1,0:T(8,128)S(1)}, f32[512,128]{1,0:T(8,128)S(1)}, f32[512,128]{1,0:T(8,128)S(1)}) custom-call(f32[4096,128]{1,0:T(8,128)} %bitcast.5, f32[4096,128]{1,0:T(8,128)} %bitcast.8), custom_call_target="tpu_custom_call" | custom-call | flops 589824 | bytes 2359296 | tf_op jit(solution)/shard_map/near/pallas_call | solution.py:113
  2.1 4.0 %collective-permute-start = (f32[512,128]{1,0:T(8,128)S(1)}, f32[512,128]{1,0:T(8,128)S(1)}, u32[]{:S(2)}, u32[]{:S(2)}) collective-permute-start(f32[512,128]{1,0:T(8,128)S(1)} %get-tuple-element.15.rest_0_), channel_id=1, source_target_pairs={{0,24},{4,28},{8,16},{12,20},{16,8},{20,12},{24,0},{28,4},{1,25},{... | collective-permute-start | bytes 786440 | tf_op jit(solution)/shard_map/ppermute | solution.py:283
  6.1 0.5 %collective-permute-start.1 = (f32[512,128]{1,0:T(8,128)S(1)}, f32[512,128]{1,0:T(8,128)S(1)}, u32[]{:S(2)}, u32[]{:S(2)}) collective-permute-start(f32[512,128]{1,0:T(8,128)S(1)} %get-tuple-element.19), channel_id=1, source_target_pairs={{0,16},{4,12},{8,24},{12,4},{16,0},{20,28},{24,8},{28,20},{1,17},{... | collective-permute-start | bytes 786440 | tf_op jit(solution)/shard_map/ppermute | solution.py:283
  6.6 0.1 collective-permute-start.2
  6.7 1.8 %far.1 = (f32[256,128]{1,0:T(8,128)S(1)}, f32[256,128]{1,0:T(8,128)S(1)}, f32[256,128]{1,0:T(8,128)S(1)}, f32[256,128]{1,0:T(8,128)S(1)}, f32[256,128]{1,0:T(8,1...) custom-call(f32[4096,128]{1,0:T(8,128)} %bitcast.6, f32[4096,128]{1,0:T(8,128)} %bitcast.9, ...), custom_call_target="tpu_custom_call" | custom-call | flops 983040 | bytes 3932160 | tf_op jit(solution)/shard_map/far/pallas_call | solution.py:113
  8.5 0.1 collective-permute-start.3
  8.6 3.0 %collective-permute-start.4 = (f32[256,128]{1,0:T(8,128)S(1)}, f32[256,128]{1,0:T(8,128)S(1)}, u32[]{:S(2)}, u32[]{:S(2)}) collective-permute-start(f32[256,128]{1,0:T(8,128)S(1)} %get-tuple-element.16.rest_0_), channel_id=1, source_target_pairs={{0,28},{4,24},{8,20},{12,16},{16,12},{20,8},{24,4},{28,0},{1,29},{... | collective-permute-start | bytes 393224 | tf_op jit(solution)/shard_map/ppermute | solution.py:283
  11.5 3.4 %update.1 = (f32[4096,128]{1,0:T(8,128)}, f32[512,128]{1,0:T(8,128)S(1)}) custom-call(f32[4096,128]{1,0:T(8,128)} %bitcast.7, f32[4096,128]{1,0:T(8,128)} %bitcast.10, f32[4096,128]{1,0:T(8,128)} %bitcast.11, f32[256,128]{1,0:T(8,128)S(1)} %get-tuple-element.16.rest_0_), custom_call_target="tpu_custom_call" | custom-call | flops 1572864 | bytes 6291456 | tf_op jit(solution)/shard_map/update/pallas_call | solution.py:159
  14.9 0.0 collective-permute-done.refs_2_.rest_1_
  14.9 0.2 collective-permute-start.5
  15.1 3.6 %collective-permute-done.1.refs_2_.rest_2_ = f32[512,128]{1,0:T(8,128)S(1)} collective-permute-done((f32[512,128]{1,0:T(8,128)S(1)}, f32[512,128]{1,0:T(8,128)S(1)}, u32[]{:S(2)}, u32[]{:S(2)}) %collective-permute-start.1) | collective-permute-done | bytes 262176 | tf_op jit(solution)/shard_map/ppermute | solution.py:283
  18.8 0.0 collective-permute-start.6
  18.8 2.5 %collective-permute-done.4.rest_6_.refs_2_ = f32[256,128]{1,0:T(8,128)S(1)} collective-permute-done((f32[256,128]{1,0:T(8,128)S(1)}, f32[256,128]{1,0:T(8,128)S(1)}, u32[]{:S(2)}, u32[]{:S(2)}) %collective-permute-start.4) | collective-permute-done | bytes 131104 | tf_op jit(solution)/shard_map/ppermute | solution.py:283
  21.2 1.9 %collective-permute-start.8 = (f32[256,128]{1,0:T(8,128)S(1)}, f32[256,128]{1,0:T(8,128)S(1)}, u32[]{:S(2)}, u32[]{:S(2)}) collective-permute-start(f32[256,128]{1,0:T(8,128)S(1)} %gate.8), channel_id=1, source_target_pairs={{0,20},{4,8},{8,28},{12,0},{16,4},{20,24},{24,12},{28,16},{1,21},{... | collective-permute-start | bytes 393224 | tf_op jit(solution)/shard_map/ppermute | solution.py:283
  23.1 0.0 collective-permute-done.2.rest_3_.refs_2_
  23.1 1.0 %collective-permute-start.7 = (f32[256,128]{1,0:T(8,128)S(1)}, f32[256,128]{1,0:T(8,128)S(1)}, u32[]{:S(2)}, u32[]{:S(2)}) collective-permute-start(f32[256,128]{1,0:T(8,128)S(1)} %gate.7), channel_id=1, source_target_pairs={{0,28},{4,24},{8,20},{12,16},{16,12},{20,8},{24,4},{28,0},{1,29},{... | collective-permute-start | bytes 393224 | tf_op jit(solution)/shard_map/ppermute | solution.py:283
  24.1 0.2 collective-permute-start.9
  24.4 0.0 collective-permute-done.6.rest_8_
  24.4 0.2 trim.2.from_ref.rest_0_
  24.6 2.0 %collective-permute-start.12 = (f32[256,128]{1,0:T(8,128)S(1)}, f32[256,128]{1,0:T(8,128)S(1)}, u32[]{:S(2)}, u32[]{:S(2)}) collective-permute-start(f32[256,128]{1,0:T(8,128)S(1)} %trim.2.from_ref.rest_0_), channel_id=1, source_target_pairs={{0,8},{4,20},{8,0},{12,28},{16,24},{20,4},{24,16},{28,12},{1,9},{5... | collective-permute-start | bytes 393224 | tf_op jit(solution)/shard_map/ppermute | solution.py:283
  26.6 2.6 %collective-permute-done.8.rest_7_ = f32[256,128]{1,0:T(8,128)S(1)} collective-permute-done((f32[256,128]{1,0:T(8,128)S(1)}, f32[256,128]{1,0:T(8,128)S(1)}, u32[]{:S(2)}, u32[]{:S(2)}) %collective-permute-start.8) | collective-permute-done | bytes 131104 | tf_op jit(solution)/shard_map/ppermute | solution.py:283
  29.2 1.0 %collective-permute-done.7.rest_6_ = f32[256,128]{1,0:T(8,128)S(1)} collective-permute-done((f32[256,128]{1,0:T(8,128)S(1)}, f32[256,128]{1,0:T(8,128)S(1)}, u32[]{:S(2)}, u32[]{:S(2)}) %collective-permute-start.7) | collective-permute-done | bytes 131104 | tf_op jit(solution)/shard_map/ppermute | solution.py:283
  30.2 0.6 %collective-permute-done.9.rest_8_ = f32[256,128]{1,0:T(8,128)S(1)} collective-permute-done((f32[256,128]{1,0:T(8,128)S(1)}, f32[256,128]{1,0:T(8,128)S(1)}, u32[]{:S(2)}, u32[]{:S(2)}) %collective-permute-start.9) | collective-permute-done | bytes 131104 | tf_op jit(solution)/shard_map/ppermute | solution.py:283
  30.8 0.2 trim.3.rest_8_
  31.1 1.5 %collective-permute-start.19 = (f32[256,128]{1,0:T(8,128)S(1)}, f32[256,128]{1,0:T(8,128)S(1)}, u32[]{:S(2)}, u32[]{:S(2)}) collective-permute-start(f32[256,128]{1,0:T(8,128)S(1)} %trim.3.rest_8_), channel_id=1, source_target_pairs={{0,8},{4,20},{8,0},{12,28},{16,24},{20,4},{24,16},{28,12},{1,9},{5... | collective-permute-start | bytes 393224 | tf_op jit(solution)/shard_map/ppermute | solution.py:283
  32.6 1.5 %collective-permute-start.10 = (f32[256,128]{1,0:T(8,128)S(1)}, f32[256,128]{1,0:T(8,128)S(1)}, u32[]{:S(2)}, u32[]{:S(2)}) collective-permute-start(f32[256,128]{1,0:T(8,128)S(1)} %trim.3.rest_8_), channel_id=1, source_target_pairs={{0,16},{4,12},{8,24},{12,4},{16,0},{20,28},{24,8},{28,20},{1,17},{... | collective-permute-start | bytes 393224 | tf_op jit(solution)/shard_map/ppermute | solution.py:283
  34.1 0.0 collective-permute-done.12.from_ref.rest_2_
  34.1 0.5 %collective-permute-start.16 = (f32[256,128]{1,0:T(8,128)S(1)}, f32[256,128]{1,0:T(8,128)S(1)}, u32[]{:S(2)}, u32[]{:S(2)}) collective-permute-start(f32[256,128]{1,0:T(8,128)S(1)} %collective-permute-done.12.from_ref.rest_2_), channel_id=1, source_target_pairs={{0,16},{4,12},{8,24},{12,4},{16,0},{20,28},{24,8},{28,20},{1,17},{... | collective-permute-start | bytes 393224 | tf_op jit(solution)/shard_map/ppermute | solution.py:283
  34.6 1.5 %collective-permute-start.14 = (f32[256,128]{1,0:T(8,128)S(1)}, f32[256,128]{1,0:T(8,128)S(1)}, u32[]{:S(2)}, u32[]{:S(2)}) collective-permute-start(f32[256,128]{1,0:T(8,128)S(1)} %trim.2.from_ref.rest_0_), channel_id=1, source_target_pairs={{0,16},{4,12},{8,24},{12,4},{16,0},{20,28},{24,8},{28,20},{1,17},{... | collective-permute-start | bytes 393224 | tf_op jit(solution)/shard_map/ppermute | solution.py:283
  36.1 0.0 collective-permute-start.18
  36.1 1.2 %collective-permute-done.19.rest_10_ = f32[256,128]{1,0:T(8,128)S(1)} collective-permute-done((f32[256,128]{1,0:T(8,128)S(1)}, f32[256,128]{1,0:T(8,128)S(1)}, u32[]{:S(2)}, u32[]{:S(2)}) %collective-permute-start.19) | collective-permute-done | bytes 131104 | tf_op jit(solution)/shard_map/ppermute | solution.py:283
  37.4 1.6 %collective-permute-start.22 = (f32[256,128]{1,0:T(8,128)S(1)}, f32[256,128]{1,0:T(8,128)S(1)}, u32[]{:S(2)}, u32[]{:S(2)}) collective-permute-start(f32[256,128]{1,0:T(8,128)S(1)} %collective-permute-done.19.rest_10_), channel_id=1, source_target_pairs={{0,16},{4,12},{8,24},{12,4},{16,0},{20,28},{24,8},{28,20},{1,17},{... | collective-permute-start | bytes 393224 | tf_op jit(solution)/shard_map/ppermute | solution.py:283
  39.0 0.1 collective-permute-done.16.from_ref.rest_6_
  39.1 0.5 %collective-permute-start.11 = (f32[256,128]{1,0:T(8,128)S(1)}, f32[256,128]{1,0:T(8,128)S(1)}, u32[]{:S(2)}, u32[]{:S(2)}) collective-permute-start(f32[256,128]{1,0:T(8,128)S(1)} %copied.4), channel_id=1, source_target_pairs={{0,4},{4,0},{8,12},{12,8},{16,20},{20,16},{24,28},{28,24},{1,5},{5... | collective-permute-start | bytes 393224 | tf_op jit(solution)/shard_map/ppermute | solution.py:283
  39.6 0.9 %collective-permute-done.14.from_ref.rest_4_ = f32[256,128]{1,0:T(8,128)S(1)} collective-permute-done((f32[256,128]{1,0:T(8,128)S(1)}, f32[256,128]{1,0:T(8,128)S(1)}, u32[]{:S(2)}, u32[]{:S(2)}) %collective-permute-start.14) | collective-permute-done | bytes 131104 | tf_op jit(solution)/shard_map/ppermute | solution.py:283
  40.5 0.6 %collective-permute-start.15 = (f32[256,128]{1,0:T(8,128)S(1)}, f32[256,128]{1,0:T(8,128)S(1)}, u32[]{:S(2)}, u32[]{:S(2)}) collective-permute-start(f32[256,128]{1,0:T(8,128)S(1)} %copied.6), channel_id=1, source_target_pairs={{0,4},{4,0},{8,12},{12,8},{16,20},{20,16},{24,28},{28,24},{1,5},{5... | collective-permute-start | bytes 393224 | tf_op jit(solution)/shard_map/ppermute | solution.py:283
  41.1 1.3 %collective-permute-done.22.rest_14_ = f32[256,128]{1,0:T(8,128)S(1)} collective-permute-done((f32[256,128]{1,0:T(8,128)S(1)}, f32[256,128]{1,0:T(8,128)S(1)}, u32[]{:S(2)}, u32[]{:S(2)}) %collective-permute-start.22) | collective-permute-done | bytes 131104 | tf_op jit(solution)/shard_map/ppermute | solution.py:283
  42.4 0.0 collective-permute-start.17
  42.4 0.0 collective-permute-done.20.rest_11_
  42.4 0.5 %collective-permute-start.21 = (f32[256,128]{1,0:T(8,128)S(1)}, f32[256,128]{1,0:T(8,128)S(1)}, u32[]{:S(2)}, u32[]{:S(2)}) collective-permute-start(f32[256,128]{1,0:T(8,128)S(1)} %collective-permute-done.10.rest_0_.rest_12_), channel_id=1, source_target_pairs={{0,4},{4,0},{8,12},{12,8},{16,20},{20,16},{24,28},{28,24},{1,5},{5... | collective-permute-start | bytes 393224 | tf_op jit(solution)/shard_map/ppermute | solution.py:283
  42.9 0.0 collective-permute-done.11.rest_1_
  42.9 0.1 collective-permute-start.23
  42.9 0.0 collective-permute-done.13.rest_3_
  42.9 0.0 collective-permute-done.15.rest_5_
  42.9 0.8 %collective-permute-done.17.rest_7_ = f32[256,128]{1,0:T(8,128)S(1)} collective-permute-done((f32[256,128]{1,0:T(8,128)S(1)}, f32[256,128]{1,0:T(8,128)S(1)}, u32[]{:S(2)}, u32[]{:S(2)}) %collective-permute-start.17) | collective-permute-done | bytes 131104 | tf_op jit(solution)/shard_map/ppermute | solution.py:283
  43.7 0.2 collective-permute-done.21.rest_13_
  43.9 0.3 collective-permute-done.23.rest_15_
  44.2 1.4 %place.1 = f32[4096,128]{1,0:T(8,128)} custom-call(f32[256,128]{1,0:T(8,128)S(1)} %trim.2.from_ref.rest_0_, f32[256,128]{1,0:T(8,128)S(1)} %collective-permute-done.11.rest_1_, f32[256,128]{1,0:T(8,128)S(1)} %collective-permute-done.12.from_ref.rest_2_, f32[256,128]{1,0:T(8,128)S(1)} %collective-permute-done.13.rest_3_, ...), custom_call_target="tpu_custom_call" | custom-call | flops 1048576 | bytes 4194304 | tf_op jit(solution)/shard_map/place/pallas_call | solution.py:222
  (15 shorter events, 0.1 us)
Async XLA Ops:
  2.1 12.8 %collective-permute-start = (f32[512,128]{1,0:T(8,128)S(1)}, f32[512,128]{1,0:T(8,128)S(1)}, u32[]{:S(2)}, u32[]{:S(2)}) collective-permute-start(f32[512,128]{1,0:T(8,128)S(1)} %get-tuple-element.15.rest_0_), channel_id=1, source_target_pairs={{0,24},{4,28},{8,16},{12,20},{16,8},{20,12},{24,0},{28,4},{1,25},{... | collective-permute-start | bytes 786440 | tf_op jit(solution)/shard_map/ppermute | solution.py:283
  6.1 12.7 %collective-permute-start.1 = (f32[512,128]{1,0:T(8,128)S(1)}, f32[512,128]{1,0:T(8,128)S(1)}, u32[]{:S(2)}, u32[]{:S(2)}) collective-permute-start(f32[512,128]{1,0:T(8,128)S(1)} %get-tuple-element.19), channel_id=1, source_target_pairs={{0,16},{4,12},{8,24},{12,4},{16,0},{20,28},{24,8},{28,20},{1,17},{... | collective-permute-start | bytes 786440 | tf_op jit(solution)/shard_map/ppermute | solution.py:283
  6.6 16.6 %collective-permute-start.2 = (f32[512,128]{1,0:T(8,128)S(1)}, f32[512,128]{1,0:T(8,128)S(1)}, u32[]{:S(2)}, u32[]{:S(2)}) collective-permute-start(f32[512,128]{1,0:T(8,128)S(1)} %get-tuple-element.20), channel_id=1, source_target_pairs={{0,8},{4,20},{8,0},{12,28},{16,24},{20,4},{24,16},{28,12},{1,9},{5... | collective-permute-start | bytes 786440 | tf_op jit(solution)/shard_map/ppermute | solution.py:283
  8.5 15.9 %collective-permute-start.3 = (f32[512,128]{1,0:T(8,128)S(1)}, f32[512,128]{1,0:T(8,128)S(1)}, u32[]{:S(2)}, u32[]{:S(2)}) collective-permute-start(f32[512,128]{1,0:T(8,128)S(1)} %get-tuple-element.21), channel_id=1, source_target_pairs={{0,4},{4,0},{8,12},{12,8},{16,20},{20,16},{24,28},{28,24},{1,5},{5... | collective-permute-start | bytes 786440 | tf_op jit(solution)/shard_map/ppermute | solution.py:283
  8.6 12.7 %collective-permute-start.4 = (f32[256,128]{1,0:T(8,128)S(1)}, f32[256,128]{1,0:T(8,128)S(1)}, u32[]{:S(2)}, u32[]{:S(2)}) collective-permute-start(f32[256,128]{1,0:T(8,128)S(1)} %get-tuple-element.16.rest_0_), channel_id=1, source_target_pairs={{0,28},{4,24},{8,20},{12,16},{16,12},{20,8},{24,4},{28,0},{1,29},{... | collective-permute-start | bytes 393224 | tf_op jit(solution)/shard_map/ppermute | solution.py:283
  14.9 9.2 %collective-permute-start.5 = (f32[256,128]{1,0:T(8,128)S(1)}, f32[256,128]{1,0:T(8,128)S(1)}, u32[]{:S(2)}, u32[]{:S(2)}) collective-permute-start(f32[256,128]{1,0:T(8,128)S(1)} %gate.5), channel_id=1, source_target_pairs={{0,20},{4,8},{8,28},{12,0},{16,4},{20,24},{24,12},{28,16},{1,21},{... | collective-permute-start | bytes 393224 | tf_op jit(solution)/shard_map/ppermute | solution.py:283
  18.8 5.6 %collective-permute-start.6 = (f32[256,128]{1,0:T(8,128)S(1)}, f32[256,128]{1,0:T(8,128)S(1)}, u32[]{:S(2)}, u32[]{:S(2)}) collective-permute-start(f32[256,128]{1,0:T(8,128)S(1)} %gate.6), channel_id=1, source_target_pairs={{0,12},{4,16},{8,4},{12,24},{16,28},{20,0},{24,20},{28,8},{1,13},{... | collective-permute-start | bytes 393224 | tf_op jit(solution)/shard_map/ppermute | solution.py:283
  21.2 8.0 %collective-permute-start.8 = (f32[256,128]{1,0:T(8,128)S(1)}, f32[256,128]{1,0:T(8,128)S(1)}, u32[]{:S(2)}, u32[]{:S(2)}) collective-permute-start(f32[256,128]{1,0:T(8,128)S(1)} %gate.8), channel_id=1, source_target_pairs={{0,20},{4,8},{8,28},{12,0},{16,4},{20,24},{24,12},{28,16},{1,21},{... | collective-permute-start | bytes 393224 | tf_op jit(solution)/shard_map/ppermute | solution.py:283
  23.1 7.1 %collective-permute-start.7 = (f32[256,128]{1,0:T(8,128)S(1)}, f32[256,128]{1,0:T(8,128)S(1)}, u32[]{:S(2)}, u32[]{:S(2)}) collective-permute-start(f32[256,128]{1,0:T(8,128)S(1)} %gate.7), channel_id=1, source_target_pairs={{0,28},{4,24},{8,20},{12,16},{16,12},{20,8},{24,4},{28,0},{1,29},{... | collective-permute-start | bytes 393224 | tf_op jit(solution)/shard_map/ppermute | solution.py:283
  24.1 6.7 %collective-permute-start.9 = (f32[256,128]{1,0:T(8,128)S(1)}, f32[256,128]{1,0:T(8,128)S(1)}, u32[]{:S(2)}, u32[]{:S(2)}) collective-permute-start(f32[256,128]{1,0:T(8,128)S(1)} %gate.9), channel_id=1, source_target_pairs={{0,12},{4,16},{8,4},{12,24},{16,28},{20,0},{24,20},{28,8},{1,13},{... | collective-permute-start | bytes 393224 | tf_op jit(solution)/shard_map/ppermute | solution.py:283
  24.6 9.5 %collective-permute-start.12 = (f32[256,128]{1,0:T(8,128)S(1)}, f32[256,128]{1,0:T(8,128)S(1)}, u32[]{:S(2)}, u32[]{:S(2)}) collective-permute-start(f32[256,128]{1,0:T(8,128)S(1)} %trim.2.from_ref.rest_0_), channel_id=1, source_target_pairs={{0,8},{4,20},{8,0},{12,28},{16,24},{20,4},{24,16},{28,12},{1,9},{5... | collective-permute-start | bytes 393224 | tf_op jit(solution)/shard_map/ppermute | solution.py:283
  31.1 6.3 %collective-permute-start.19 = (f32[256,128]{1,0:T(8,128)S(1)}, f32[256,128]{1,0:T(8,128)S(1)}, u32[]{:S(2)}, u32[]{:S(2)}) collective-permute-start(f32[256,128]{1,0:T(8,128)S(1)} %trim.3.rest_8_), channel_id=1, source_target_pairs={{0,8},{4,20},{8,0},{12,28},{16,24},{20,4},{24,16},{28,12},{1,9},{5... | collective-permute-start | bytes 393224 | tf_op jit(solution)/shard_map/ppermute | solution.py:283
  32.6 6.4 %collective-permute-start.10 = (f32[256,128]{1,0:T(8,128)S(1)}, f32[256,128]{1,0:T(8,128)S(1)}, u32[]{:S(2)}, u32[]{:S(2)}) collective-permute-start(f32[256,128]{1,0:T(8,128)S(1)} %trim.3.rest_8_), channel_id=1, source_target_pairs={{0,16},{4,12},{8,24},{12,4},{16,0},{20,28},{24,8},{28,20},{1,17},{... | collective-permute-start | bytes 393224 | tf_op jit(solution)/shard_map/ppermute | solution.py:283
  34.1 5.0 %collective-permute-start.16 = (f32[256,128]{1,0:T(8,128)S(1)}, f32[256,128]{1,0:T(8,128)S(1)}, u32[]{:S(2)}, u32[]{:S(2)}) collective-permute-start(f32[256,128]{1,0:T(8,128)S(1)} %collective-permute-done.12.from_ref.rest_2_), channel_id=1, source_target_pairs={{0,16},{4,12},{8,24},{12,4},{16,0},{20,28},{24,8},{28,20},{1,17},{... | collective-permute-start | bytes 393224 | tf_op jit(solution)/shard_map/ppermute | solution.py:283
  34.6 5.9 %collective-permute-start.14 = (f32[256,128]{1,0:T(8,128)S(1)}, f32[256,128]{1,0:T(8,128)S(1)}, u32[]{:S(2)}, u32[]{:S(2)}) collective-permute-start(f32[256,128]{1,0:T(8,128)S(1)} %trim.2.from_ref.rest_0_), channel_id=1, source_target_pairs={{0,16},{4,12},{8,24},{12,4},{16,0},{20,28},{24,8},{28,20},{1,17},{... | collective-permute-start | bytes 393224 | tf_op jit(solution)/shard_map/ppermute | solution.py:283
  36.1 4.4 %collective-permute-start.18 = (f32[256,128]{1,0:T(8,128)S(1)}, f32[256,128]{1,0:T(8,128)S(1)}, u32[]{:S(2)}, u32[]{:S(2)}) collective-permute-start(f32[256,128]{1,0:T(8,128)S(1)} %trim.3.rest_8_), channel_id=1, source_target_pairs={{0,4},{4,0},{8,12},{12,8},{16,20},{20,16},{24,28},{28,24},{1,5},{5... | collective-permute-start | bytes 393224 | tf_op jit(solution)/shard_map/ppermute | solution.py:283
  37.4 5.0 %collective-permute-start.22 = (f32[256,128]{1,0:T(8,128)S(1)}, f32[256,128]{1,0:T(8,128)S(1)}, u32[]{:S(2)}, u32[]{:S(2)}) collective-permute-start(f32[256,128]{1,0:T(8,128)S(1)} %collective-permute-done.19.rest_10_), channel_id=1, source_target_pairs={{0,16},{4,12},{8,24},{12,4},{16,0},{20,28},{24,8},{28,20},{1,17},{... | collective-permute-start | bytes 393224 | tf_op jit(solution)/shard_map/ppermute | solution.py:283
  39.0 3.4 %collective-permute-start.20 = (f32[256,128]{1,0:T(8,128)S(1)}, f32[256,128]{1,0:T(8,128)S(1)}, u32[]{:S(2)}, u32[]{:S(2)}) collective-permute-start(f32[256,128]{1,0:T(8,128)S(1)} %collective-permute-done.19.rest_10_), channel_id=1, source_target_pairs={{0,4},{4,0},{8,12},{12,8},{16,20},{20,16},{24,28},{28,24},{1,5},{5... | collective-permute-start | bytes 393224 | tf_op jit(solution)/shard_map/ppermute | solution.py:283
  39.1 3.8 %collective-permute-start.11 = (f32[256,128]{1,0:T(8,128)S(1)}, f32[256,128]{1,0:T(8,128)S(1)}, u32[]{:S(2)}, u32[]{:S(2)}) collective-permute-start(f32[256,128]{1,0:T(8,128)S(1)} %copied.4), channel_id=1, source_target_pairs={{0,4},{4,0},{8,12},{12,8},{16,20},{20,16},{24,28},{28,24},{1,5},{5... | collective-permute-start | bytes 393224 | tf_op jit(solution)/shard_map/ppermute | solution.py:283
  40.5 2.5 %collective-permute-start.13 = (f32[256,128]{1,0:T(8,128)S(1)}, f32[256,128]{1,0:T(8,128)S(1)}, u32[]{:S(2)}, u32[]{:S(2)}) collective-permute-start(f32[256,128]{1,0:T(8,128)S(1)} %copied.5), channel_id=1, source_target_pairs={{0,4},{4,0},{8,12},{12,8},{16,20},{20,16},{24,28},{28,24},{1,5},{5... | collective-permute-start | bytes 393224 | tf_op jit(solution)/shard_map/ppermute | solution.py:283
  40.5 2.4 %collective-permute-start.15 = (f32[256,128]{1,0:T(8,128)S(1)}, f32[256,128]{1,0:T(8,128)S(1)}, u32[]{:S(2)}, u32[]{:S(2)}) collective-permute-start(f32[256,128]{1,0:T(8,128)S(1)} %copied.6), channel_id=1, source_target_pairs={{0,4},{4,0},{8,12},{12,8},{16,20},{20,16},{24,28},{28,24},{1,5},{5... | collective-permute-start | bytes 393224 | tf_op jit(solution)/shard_map/ppermute | solution.py:283
  42.4 1.3 %collective-permute-start.17 = (f32[256,128]{1,0:T(8,128)S(1)}, f32[256,128]{1,0:T(8,128)S(1)}, u32[]{:S(2)}, u32[]{:S(2)}) collective-permute-start(f32[256,128]{1,0:T(8,128)S(1)} %copied.7), channel_id=1, source_target_pairs={{0,4},{4,0},{8,12},{12,8},{16,20},{20,16},{24,28},{28,24},{1,5},{5... | collective-permute-start | bytes 393224 | tf_op jit(solution)/shard_map/ppermute | solution.py:283
  42.4 1.5 %collective-permute-start.21 = (f32[256,128]{1,0:T(8,128)S(1)}, f32[256,128]{1,0:T(8,128)S(1)}, u32[]{:S(2)}, u32[]{:S(2)}) collective-permute-start(f32[256,128]{1,0:T(8,128)S(1)} %collective-permute-done.10.rest_0_.rest_12_), channel_id=1, source_target_pairs={{0,4},{4,0},{8,12},{12,8},{16,20},{20,16},{24,28},{28,24},{1,5},{5... | collective-permute-start | bytes 393224 | tf_op jit(solution)/shard_map/ppermute | solution.py:283
  42.9 1.3 %collective-permute-start.23 = (f32[256,128]{1,0:T(8,128)S(1)}, f32[256,128]{1,0:T(8,128)S(1)}, u32[]{:S(2)}, u32[]{:S(2)}) collective-permute-start(f32[256,128]{1,0:T(8,128)S(1)} %collective-permute-done.22.rest_14_), channel_id=1, source_target_pairs={{0,4},{4,0},{8,12},{12,8},{16,20},{20,16},{24,28},{28,24},{1,5},{5... | collective-permute-start | bytes 393224 | tf_op jit(solution)/shard_map/ppermute | solution.py:283

commit v3 on v2

--- a/solution.py
+++ b/solution.py
@@ -9,7 +9,7 @@
 
 LANES = 128
 DEPTH = 4
-LATER = 2
+WAIT = 1
 CORES = 2
 
 
@@ -231,22 +231,6 @@
     )(*blocks.values())
 
 
-def copy_kernel(from_ref, *rest):
-    rest[-1][...] = from_ref[...]
-
-
-def copied(block, deps):
-    return pl.pallas_call(
-        copy_kernel,
-        out_shape=jax.ShapeDtypeStruct(block.shape, jnp.float32),
-        in_specs=[VMEM] + [ANY] * len(deps),
-        out_specs=VMEM,
-        compiler_params=pltpu.CompilerParams(vmem_limit_bytes=16 << 20),
-        cost_estimate=cost(2 * block.size),
-        name="copied",
-    )(block, *deps)
-
-
 def gate_kernel(*refs):
     del refs
 
@@ -288,7 +272,7 @@
         return queue[-1]
 
     far_chips = list(range(chips - 1, 0, -1))
-    near_routes = [(label, 0) for label in far_chips]
+    near_routes = [(label, 0) for label in range(1, chips)]
     far_routes = [(label, 1) for label in far_chips]
     near = send_blocks(m, g, workers, near_routes, [[0, rows]] * len(near_routes), [], "near")
     held = [queued(block, route) for route, block in zip(near_routes, near)]
@@ -304,8 +288,9 @@
             got[part].append(queued(sends[2 * i + part], route, *([] if early else [own_w])))
 
     gathered = []
-    for got, (low, high) in zip(got, parts):
-        new = [trim(own_w, held + got, low, high, [], "trim")]
+    for part, (low, high) in enumerate(parts):
+        deps = got[1][:WAIT] if part == 0 else []
+        new = [trim(own_w, held + got[part], low, high, deps, "trim")]
         for label in range(1, chips):
             step = 1 << label.bit_length() - 1
             if chips & (chips - 1) == 0:
@@ -317,8 +302,6 @@
     for new, (low, high) in zip(gathered, parts):
         for label, block in enumerate(new):
             blocks[low, label, 0] = block
-            if low == 0:
-                block = copied(block, [gathered[1][min(LATER, chips - 1)]])
             blocks[low, label, 1] = send(block, (0, 1))
     result = place(blocks, workers, rows)
     return updated.reshape(momentum.shape), result.reshape(weights.shape)

time: 45.8 us -> 44 us (0.961)
  waiting for transfers between devices: 15 us -> 11.9 us
  starting transfers between devices: 21.3 us -> 22.7 us
    ppermute x24, waiting for transfers between devices: 15 us -> 11.9 us  [send(): return lax.ppermute(block, 'worker', pairs)]
    ppermute x24, starting transfers between devices: 21.3 us -> 22.7 us  [send(): return lax.ppermute(block, 'worker', pairs)]
  transfers between devices with their start and end apart: 24 -> 24, of which waited for: 12 -> 9; matrix products, arithmetic and copies ran while one was open for 0% -> 0% of each run, Pallas kernels for 12% -> 13%
where the time goes in v3:
time: 44 us; the launch traced here: 43.9 us
  starting transfers between devices  22.7 us (52%)
  waiting for transfers between devices  11.9 us (27%)
  Pallas kernels  8.54 us (19%)
  between operations  0.73 us (2%)
    ppermute x24, starting transfers between devices, send(): return lax.ppermute(block, 'worker', pairs)  22.7 us
    ppermute x24, waiting for transfers between devices, send(): return lax.ppermute(block, 'worker', pairs)  11.9 us
    pallas_call x1, Pallas kernels, update(): pl.pallas_call(functools.partial(update_kernel, workers, pieces, rows, le...  3.37 us
    pallas_call x2, Pallas kernels, send_blocks(): pl.pallas_call(functools.partial(send_kernel, workers, routes, cuts, rows...  3.23 us
    pallas_call x1, Pallas kernels, place(): pl.pallas_call(functools.partial(place_kernel, workers, rows, list(blocks...  1.44 us
  transfers between devices with their start and end apart: 24, of which 9 were waited for; matrix products, arithmetic and copies ran while one was open for 0% of the time, Pallas kernels for 13%

profile of v3, /device:TPU:0, one launch (start us, length us, event | category | flops | bytes accessed | tf_op | source)
XLA Modules:
  0.0 43.9 jit_solution(3549357666385451448)
XLA Ops:
  0.6 1.5 %near.1 = (f32[512,128]{1,0:T(8,128)S(1)}, f32[512,128]{1,0:T(8,128)S(1)}, f32[512,128]{1,0:T(8,128)S(1)}) custom-call(f32[4096,128]{1,0:T(8,128)} %bitcast.5, f32[4096,128]{1,0:T(8,128)} %bitcast.8), custom_call_target="tpu_custom_call" | custom-call | flops 589824 | bytes 2359296 | tf_op jit(solution)/shard_map/near/pallas_call | solution.py:113
  2.1 3.0 %collective-permute-start = (f32[512,128]{1,0:T(8,128)S(1)}, f32[512,128]{1,0:T(8,128)S(1)}, u32[]{:S(2)}, u32[]{:S(2)}) collective-permute-start(f32[512,128]{1,0:T(8,128)S(1)} %get-tuple-element.15.rest_0_), channel_id=1, source_target_pairs={{0,8},{4,20},{8,0},{12,28},{16,24},{20,4},{24,16},{28,12},{1,9},{5... | collective-permute-start | bytes 786440 | tf_op jit(solution)/shard_map/ppermute | solution.py:267
  5.1 1.5 %collective-permute-start.1 = (f32[512,128]{1,0:T(8,128)S(1)}, f32[512,128]{1,0:T(8,128)S(1)}, u32[]{:S(2)}, u32[]{:S(2)}) collective-permute-start(f32[512,128]{1,0:T(8,128)S(1)} %get-tuple-element.19), channel_id=1, source_target_pairs={{0,16},{4,12},{8,24},{12,4},{16,0},{20,28},{24,8},{28,20},{1,17},{... | collective-permute-start | bytes 786440 | tf_op jit(solution)/shard_map/ppermute | solution.py:267
  6.6 0.0 collective-permute-start.2
  6.6 1.8 %far.1 = (f32[256,128]{1,0:T(8,128)S(1)}, f32[256,128]{1,0:T(8,128)S(1)}, f32[256,128]{1,0:T(8,128)S(1)}, f32[256,128]{1,0:T(8,128)S(1)}, f32[256,128]{1,0:T(8,1...) custom-call(f32[4096,128]{1,0:T(8,128)} %bitcast.6, f32[4096,128]{1,0:T(8,128)} %bitcast.9, ...), custom_call_target="tpu_custom_call" | custom-call | flops 983040 | bytes 3932160 | tf_op jit(solution)/shard_map/far/pallas_call | solution.py:113
  8.4 1.6 %collective-permute-start.4 = (f32[256,128]{1,0:T(8,128)S(1)}, f32[256,128]{1,0:T(8,128)S(1)}, u32[]{:S(2)}, u32[]{:S(2)}) collective-permute-start(f32[256,128]{1,0:T(8,128)S(1)} %get-tuple-element.16.rest_0_), channel_id=1, source_target_pairs={{0,28},{4,24},{8,20},{12,16},{16,12},{20,8},{24,4},{28,0},{1,29},{... | collective-permute-start | bytes 393224 | tf_op jit(solution)/shard_map/ppermute | solution.py:267
  10.0 1.5 %collective-permute-start.3 = (f32[512,128]{1,0:T(8,128)S(1)}, f32[512,128]{1,0:T(8,128)S(1)}, u32[]{:S(2)}, u32[]{:S(2)}) collective-permute-start(f32[512,128]{1,0:T(8,128)S(1)} %get-tuple-element.21), channel_id=1, source_target_pairs={{0,4},{4,0},{8,12},{12,8},{16,20},{20,16},{24,28},{28,24},{1,5},{5... | collective-permute-start | bytes 786440 | tf_op jit(solution)/shard_map/ppermute | solution.py:267
  11.5 3.4 %update.1 = (f32[4096,128]{1,0:T(8,128)}, f32[512,128]{1,0:T(8,128)S(1)}) custom-call(f32[4096,128]{1,0:T(8,128)} %bitcast.7, f32[4096,128]{1,0:T(8,128)} %bitcast.10, f32[4096,128]{1,0:T(8,128)} %bitcast.11, f32[256,128]{1,0:T(8,128)S(1)} %get-tuple-element.16.rest_0_), custom_call_target="tpu_custom_call" | custom-call | flops 1572864 | bytes 6291456 | tf_op jit(solution)/shard_map/update/pallas_call | solution.py:159
  14.9 0.0 collective-permute-done.refs_2_.rest_1_
  14.9 0.2 collective-permute-start.5
  15.1 0.0 collective-permute-done.1.refs_2_.rest_2_
  15.1 1.6 %collective-permute-start.6 = (f32[256,128]{1,0:T(8,128)S(1)}, f32[256,128]{1,0:T(8,128)S(1)}, u32[]{:S(2)}, u32[]{:S(2)}) collective-permute-start(f32[256,128]{1,0:T(8,128)S(1)} %gate.6), channel_id=1, source_target_pairs={{0,12},{4,16},{8,4},{12,24},{16,28},{20,0},{24,20},{28,8},{1,13},{... | collective-permute-start | bytes 393224 | tf_op jit(solution)/shard_map/ppermute | solution.py:267
  16.7 2.8 %collective-permute-done.2.refs_2_.rest_3_ = f32[512,128]{1,0:T(8,128)S(1)} collective-permute-done((f32[512,128]{1,0:T(8,128)S(1)}, f32[512,128]{1,0:T(8,128)S(1)}, u32[]{:S(2)}, u32[]{:S(2)}) %collective-permute-start.2) | collective-permute-done | bytes 262176 | tf_op jit(solution)/shard_map/ppermute | solution.py:267
  19.5 1.0 %collective-permute-start.7 = (f32[256,128]{1,0:T(8,128)S(1)}, f32[256,128]{1,0:T(8,128)S(1)}, u32[]{:S(2)}, u32[]{:S(2)}) collective-permute-start(f32[256,128]{1,0:T(8,128)S(1)} %gate.7), channel_id=1, source_target_pairs={{0,28},{4,24},{8,20},{12,16},{16,12},{20,8},{24,4},{28,0},{1,29},{... | collective-permute-start | bytes 393224 | tf_op jit(solution)/shard_map/ppermute | solution.py:267
  20.5 0.0 collective-permute-done.4.rest_6_.refs_2_
  20.5 1.7 %collective-permute-start.15 = (f32[256,128]{1,0:T(8,128)S(1)}, f32[256,128]{1,0:T(8,128)S(1)}, u32[]{:S(2)}, u32[]{:S(2)}) collective-permute-start(f32[256,128]{1,0:T(8,128)S(1)} %gate.8), channel_id=1, source_target_pairs={{0,20},{4,8},{8,28},{12,0},{16,4},{20,24},{24,12},{28,16},{1,21},{... | collective-permute-start | bytes 393224 | tf_op jit(solution)/shard_map/ppermute | solution.py:267
  22.1 2.0 %collective-permute-done.5.rest_7_.refs_2_ = f32[256,128]{1,0:T(8,128)S(1)} collective-permute-done((f32[256,128]{1,0:T(8,128)S(1)}, f32[256,128]{1,0:T(8,128)S(1)}, u32[]{:S(2)}, u32[]{:S(2)}) %collective-permute-start.5) | collective-permute-done | bytes 131104 | tf_op jit(solution)/shard_map/ppermute | solution.py:267
  24.1 1.8 %collective-permute-start.16 = (f32[256,128]{1,0:T(8,128)S(1)}, f32[256,128]{1,0:T(8,128)S(1)}, u32[]{:S(2)}, u32[]{:S(2)}) collective-permute-start(f32[256,128]{1,0:T(8,128)S(1)} %gate.9), channel_id=1, source_target_pairs={{0,12},{4,16},{8,4},{12,24},{16,28},{20,0},{24,20},{28,8},{1,13},{... | collective-permute-start | bytes 393224 | tf_op jit(solution)/shard_map/ppermute | solution.py:267
  26.0 0.0 collective-permute-done.6.rest_8_
  26.0 0.4 collective-permute-done.7.rest_9_.rest_6_
  26.3 0.2 trim.2.rest_0_
  26.6 1.7 %collective-permute-start.11 = (f32[256,128]{1,0:T(8,128)S(1)}, f32[256,128]{1,0:T(8,128)S(1)}, u32[]{:S(2)}, u32[]{:S(2)}) collective-permute-start(f32[256,128]{1,0:T(8,128)S(1)} %trim.2.rest_0_), channel_id=1, source_target_pairs={{0,16},{4,12},{8,24},{12,4},{16,0},{20,28},{24,8},{28,20},{1,17},{... | collective-permute-start | bytes 393224 | tf_op jit(solution)/shard_map/ppermute | solution.py:267
  28.2 2.0 %collective-permute-start.9 = (f32[256,128]{1,0:T(8,128)S(1)}, f32[256,128]{1,0:T(8,128)S(1)}, u32[]{:S(2)}, u32[]{:S(2)}) collective-permute-start(f32[256,128]{1,0:T(8,128)S(1)} %trim.2.rest_0_), channel_id=1, source_target_pairs={{0,8},{4,20},{8,0},{12,28},{16,24},{20,4},{24,16},{28,12},{1,9},{5... | collective-permute-start | bytes 393224 | tf_op jit(solution)/shard_map/ppermute | solution.py:267
  30.3 0.0 collective-permute-done.15.rest_7_
  30.3 0.0 collective-permute-done.16.rest_8_
  30.3 0.3 trim.3.rest_8_
  30.5 1.0 %collective-permute-start.18 = (f32[256,128]{1,0:T(8,128)S(1)}, f32[256,128]{1,0:T(8,128)S(1)}, u32[]{:S(2)}, u32[]{:S(2)}) collective-permute-start(f32[256,128]{1,0:T(8,128)S(1)} %trim.3.rest_8_), channel_id=1, source_target_pairs={{0,8},{4,20},{8,0},{12,28},{16,24},{20,4},{24,16},{28,12},{1,9},{5... | collective-permute-start | bytes 393224 | tf_op jit(solution)/shard_map/ppermute | solution.py:267
  31.5 0.1 collective-permute-done.11.rest_4_
  31.6 0.0 collective-permute-start.12
  31.6 1.6 %collective-permute-done.9.rest_2_ = f32[256,128]{1,0:T(8,128)S(1)} collective-permute-done((f32[256,128]{1,0:T(8,128)S(1)}, f32[256,128]{1,0:T(8,128)S(1)}, u32[]{:S(2)}, u32[]{:S(2)}) %collective-permute-start.9) | collective-permute-done | bytes 131104 | tf_op jit(solution)/shard_map/ppermute | solution.py:267
  33.2 0.7 %collective-permute-start.13 = (f32[256,128]{1,0:T(8,128)S(1)}, f32[256,128]{1,0:T(8,128)S(1)}, u32[]{:S(2)}, u32[]{:S(2)}) collective-permute-start(f32[256,128]{1,0:T(8,128)S(1)} %collective-permute-done.9.rest_2_), channel_id=1, source_target_pairs={{0,16},{4,12},{8,24},{12,4},{16,0},{20,28},{24,8},{28,20},{1,17},{... | collective-permute-start | bytes 393224 | tf_op jit(solution)/shard_map/ppermute | solution.py:267
  33.9 0.8 %collective-permute-start.10 = (f32[256,128]{1,0:T(8,128)S(1)}, f32[256,128]{1,0:T(8,128)S(1)}, u32[]{:S(2)}, u32[]{:S(2)}) collective-permute-start(f32[256,128]{1,0:T(8,128)S(1)} %collective-permute-done.9.rest_2_), channel_id=1, source_target_pairs={{0,4},{4,0},{8,12},{12,8},{16,20},{20,16},{24,28},{28,24},{1,5},{5... | collective-permute-start | bytes 393224 | tf_op jit(solution)/shard_map/ppermute | solution.py:267
  34.7 0.0 collective-permute-done.8.rest_1_
  34.7 1.3 %collective-permute-start.20 = (f32[256,128]{1,0:T(8,128)S(1)}, f32[256,128]{1,0:T(8,128)S(1)}, u32[]{:S(2)}, u32[]{:S(2)}) collective-permute-start(f32[256,128]{1,0:T(8,128)S(1)} %trim.3.rest_8_), channel_id=1, source_target_pairs={{0,16},{4,12},{8,24},{12,4},{16,0},{20,28},{24,8},{28,20},{1,17},{... | collective-permute-start | bytes 393224 | tf_op jit(solution)/shard_map/ppermute | solution.py:267
  36.0 0.0 collective-permute-done.18.rest_10_
  36.0 0.8 %collective-permute-start.22 = (f32[256,128]{1,0:T(8,128)S(1)}, f32[256,128]{1,0:T(8,128)S(1)}, u32[]{:S(2)}, u32[]{:S(2)}) collective-permute-start(f32[256,128]{1,0:T(8,128)S(1)} %collective-permute-done.18.rest_10_), channel_id=1, source_target_pairs={{0,16},{4,12},{8,24},{12,4},{16,0},{20,28},{24,8},{28,20},{1,17},{... | collective-permute-start | bytes 393224 | tf_op jit(solution)/shard_map/ppermute | solution.py:267
  36.7 0.0 collective-permute-done.12.rest_5_
  36.7 0.0 collective-permute-start.17
  36.7 1.4 %collective-permute-done.13.rest_6_ = f32[256,128]{1,0:T(8,128)S(1)} collective-permute-done((f32[256,128]{1,0:T(8,128)S(1)}, f32[256,128]{1,0:T(8,128)S(1)}, u32[]{:S(2)}, u32[]{:S(2)}) %collective-permute-start.13) | collective-permute-done | bytes 131104 | tf_op jit(solution)/shard_map/ppermute | solution.py:267
  38.2 0.0 collective-permute-start.19
  38.2 0.0 collective-permute-done.10.rest_3_
  38.2 0.5 %collective-permute-start.14 = (f32[256,128]{1,0:T(8,128)S(1)}, f32[256,128]{1,0:T(8,128)S(1)}, u32[]{:S(2)}, u32[]{:S(2)}) collective-permute-start(f32[256,128]{1,0:T(8,128)S(1)} %collective-permute-done.13.rest_6_), channel_id=1, source_target_pairs={{0,4},{4,0},{8,12},{12,8},{16,20},{20,16},{24,28},{28,24},{1,5},{5... | collective-permute-start | bytes 393224 | tf_op jit(solution)/shard_map/ppermute | solution.py:267
  38.7 1.0 %collective-permute-done.20.rest_12_ = f32[256,128]{1,0:T(8,128)S(1)} collective-permute-done((f32[256,128]{1,0:T(8,128)S(1)}, f32[256,128]{1,0:T(8,128)S(1)}, u32[]{:S(2)}, u32[]{:S(2)}) %collective-permute-start.20) | collective-permute-done | bytes 131104 | tf_op jit(solution)/shard_map/ppermute | solution.py:267
  39.7 0.0 collective-permute-start.21
  39.7 1.4 %collective-permute-done.22.rest_14_ = f32[256,128]{1,0:T(8,128)S(1)} collective-permute-done((f32[256,128]{1,0:T(8,128)S(1)}, f32[256,128]{1,0:T(8,128)S(1)}, u32[]{:S(2)}, u32[]{:S(2)}) %collective-permute-start.22) | collective-permute-done | bytes 131104 | tf_op jit(solution)/shard_map/ppermute | solution.py:267
  41.1 0.0 collective-permute-done.21.rest_13_
  41.1 1.3 %collective-permute-done.23.rest_15_ = f32[256,128]{1,0:T(8,128)S(1)} collective-permute-done((f32[256,128]{1,0:T(8,128)S(1)}, f32[256,128]{1,0:T(8,128)S(1)}, u32[]{:S(2)}, u32[]{:S(2)}) %collective-permute-start.23) | collective-permute-done | bytes 131104 | tf_op jit(solution)/shard_map/ppermute | solution.py:267
  42.4 1.4 %place.1 = f32[4096,128]{1,0:T(8,128)} custom-call(f32[256,128]{1,0:T(8,128)S(1)} %trim.2.rest_0_, f32[256,128]{1,0:T(8,128)S(1)} %collective-permute-done.8.rest_1_, f32[256,128]{1,0:T(8,128)S(1)} %collective-permute-done.9.rest_2_, f32[256,128]{1,0:T(8,128)S(1)} %collective-permute-done.10.rest_3_, f32[256,128]{1,0:T(8,128)S(1)} %collective-permute-done.11.rest_4_, ...), custom_call_target="tpu_custom_call" | custom-call | flops 1048576 | bytes 4194304 | tf_op jit(solution)/shard_map/place/pallas_call | solution.py:222
  (11 shorter events, 0.0 us)
Async XLA Ops:
  2.1 12.8 %collective-permute-start = (f32[512,128]{1,0:T(8,128)S(1)}, f32[512,128]{1,0:T(8,128)S(1)}, u32[]{:S(2)}, u32[]{:S(2)}) collective-permute-start(f32[512,128]{1,0:T(8,128)S(1)} %get-tuple-element.15.rest_0_), channel_id=1, source_target_pairs={{0,8},{4,20},{8,0},{12,28},{16,24},{20,4},{24,16},{28,12},{1,9},{5... | collective-permute-start | bytes 786440 | tf_op jit(solution)/shard_map/ppermute | solution.py:267
  5.1 10.0 %collective-permute-start.1 = (f32[512,128]{1,0:T(8,128)S(1)}, f32[512,128]{1,0:T(8,128)S(1)}, u32[]{:S(2)}, u32[]{:S(2)}) collective-permute-start(f32[512,128]{1,0:T(8,128)S(1)} %get-tuple-element.19), channel_id=1, source_target_pairs={{0,16},{4,12},{8,24},{12,4},{16,0},{20,28},{24,8},{28,20},{1,17},{... | collective-permute-start | bytes 786440 | tf_op jit(solution)/shard_map/ppermute | solution.py:267
  6.6 12.8 %collective-permute-start.2 = (f32[512,128]{1,0:T(8,128)S(1)}, f32[512,128]{1,0:T(8,128)S(1)}, u32[]{:S(2)}, u32[]{:S(2)}) collective-permute-start(f32[512,128]{1,0:T(8,128)S(1)} %get-tuple-element.20), channel_id=1, source_target_pairs={{0,24},{4,28},{8,16},{12,20},{16,8},{20,12},{24,0},{28,4},{1,25},{... | collective-permute-start | bytes 786440 | tf_op jit(solution)/shard_map/ppermute | solution.py:267
  8.4 12.0 %collective-permute-start.4 = (f32[256,128]{1,0:T(8,128)S(1)}, f32[256,128]{1,0:T(8,128)S(1)}, u32[]{:S(2)}, u32[]{:S(2)}) collective-permute-start(f32[256,128]{1,0:T(8,128)S(1)} %get-tuple-element.16.rest_0_), channel_id=1, source_target_pairs={{0,28},{4,24},{8,20},{12,16},{16,12},{20,8},{24,4},{28,0},{1,29},{... | collective-permute-start | bytes 393224 | tf_op jit(solution)/shard_map/ppermute | solution.py:267
  10.0 16.0 %collective-permute-start.3 = (f32[512,128]{1,0:T(8,128)S(1)}, f32[512,128]{1,0:T(8,128)S(1)}, u32[]{:S(2)}, u32[]{:S(2)}) collective-permute-start(f32[512,128]{1,0:T(8,128)S(1)} %get-tuple-element.21), channel_id=1, source_target_pairs={{0,4},{4,0},{8,12},{12,8},{16,20},{20,16},{24,28},{28,24},{1,5},{5... | collective-permute-start | bytes 786440 | tf_op jit(solution)/shard_map/ppermute | solution.py:267
  14.9 9.2 %collective-permute-start.5 = (f32[256,128]{1,0:T(8,128)S(1)}, f32[256,128]{1,0:T(8,128)S(1)}, u32[]{:S(2)}, u32[]{:S(2)}) collective-permute-start(f32[256,128]{1,0:T(8,128)S(1)} %gate.5), channel_id=1, source_target_pairs={{0,20},{4,8},{8,28},{12,0},{16,4},{20,24},{24,12},{28,16},{1,21},{... | collective-permute-start | bytes 393224 | tf_op jit(solution)/shard_map/ppermute | solution.py:267
  15.1 10.9 %collective-permute-start.6 = (f32[256,128]{1,0:T(8,128)S(1)}, f32[256,128]{1,0:T(8,128)S(1)}, u32[]{:S(2)}, u32[]{:S(2)}) collective-permute-start(f32[256,128]{1,0:T(8,128)S(1)} %gate.6), channel_id=1, source_target_pairs={{0,12},{4,16},{8,4},{12,24},{16,28},{20,0},{24,20},{28,8},{1,13},{... | collective-permute-start | bytes 393224 | tf_op jit(solution)/shard_map/ppermute | solution.py:267
  19.5 6.9 %collective-permute-start.7 = (f32[256,128]{1,0:T(8,128)S(1)}, f32[256,128]{1,0:T(8,128)S(1)}, u32[]{:S(2)}, u32[]{:S(2)}) collective-permute-start(f32[256,128]{1,0:T(8,128)S(1)} %gate.7), channel_id=1, source_target_pairs={{0,28},{4,24},{8,20},{12,16},{16,12},{20,8},{24,4},{28,0},{1,29},{... | collective-permute-start | bytes 393224 | tf_op jit(solution)/shard_map/ppermute | solution.py:267
  20.5 9.8 %collective-permute-start.15 = (f32[256,128]{1,0:T(8,128)S(1)}, f32[256,128]{1,0:T(8,128)S(1)}, u32[]{:S(2)}, u32[]{:S(2)}) collective-permute-start(f32[256,128]{1,0:T(8,128)S(1)} %gate.8), channel_id=1, source_target_pairs={{0,20},{4,8},{8,28},{12,0},{16,4},{20,24},{24,12},{28,16},{1,21},{... | collective-permute-start | bytes 393224 | tf_op jit(solution)/shard_map/ppermute | solution.py:267
  24.1 6.1 %collective-permute-start.16 = (f32[256,128]{1,0:T(8,128)S(1)}, f32[256,128]{1,0:T(8,128)S(1)}, u32[]{:S(2)}, u32[]{:S(2)}) collective-permute-start(f32[256,128]{1,0:T(8,128)S(1)} %gate.9), channel_id=1, source_target_pairs={{0,12},{4,16},{8,4},{12,24},{16,28},{20,0},{24,20},{28,8},{1,13},{... | collective-permute-start | bytes 393224 | tf_op jit(solution)/shard_map/ppermute | solution.py:267
  26.6 5.0 %collective-permute-start.11 = (f32[256,128]{1,0:T(8,128)S(1)}, f32[256,128]{1,0:T(8,128)S(1)}, u32[]{:S(2)}, u32[]{:S(2)}) collective-permute-start(f32[256,128]{1,0:T(8,128)S(1)} %trim.2.rest_0_), channel_id=1, source_target_pairs={{0,16},{4,12},{8,24},{12,4},{16,0},{20,28},{24,8},{28,20},{1,17},{... | collective-permute-start | bytes 393224 | tf_op jit(solution)/shard_map/ppermute | solution.py:267
  28.2 5.0 %collective-permute-start.9 = (f32[256,128]{1,0:T(8,128)S(1)}, f32[256,128]{1,0:T(8,128)S(1)}, u32[]{:S(2)}, u32[]{:S(2)}) collective-permute-start(f32[256,128]{1,0:T(8,128)S(1)} %trim.2.rest_0_), channel_id=1, source_target_pairs={{0,8},{4,20},{8,0},{12,28},{16,24},{20,4},{24,16},{28,12},{1,9},{5... | collective-permute-start | bytes 393224 | tf_op jit(solution)/shard_map/ppermute | solution.py:267
  30.3 4.4 %collective-permute-start.8 = (f32[256,128]{1,0:T(8,128)S(1)}, f32[256,128]{1,0:T(8,128)S(1)}, u32[]{:S(2)}, u32[]{:S(2)}) collective-permute-start(f32[256,128]{1,0:T(8,128)S(1)} %trim.2.rest_0_), channel_id=1, source_target_pairs={{0,4},{4,0},{8,12},{12,8},{16,20},{20,16},{24,28},{28,24},{1,5},{5... | collective-permute-start | bytes 393224 | tf_op jit(solution)/shard_map/ppermute | solution.py:267
  30.5 5.4 %collective-permute-start.18 = (f32[256,128]{1,0:T(8,128)S(1)}, f32[256,128]{1,0:T(8,128)S(1)}, u32[]{:S(2)}, u32[]{:S(2)}) collective-permute-start(f32[256,128]{1,0:T(8,128)S(1)} %trim.3.rest_8_), channel_id=1, source_target_pairs={{0,8},{4,20},{8,0},{12,28},{16,24},{20,4},{24,16},{28,12},{1,9},{5... | collective-permute-start | bytes 393224 | tf_op jit(solution)/shard_map/ppermute | solution.py:267
  31.6 5.1 %collective-permute-start.12 = (f32[256,128]{1,0:T(8,128)S(1)}, f32[256,128]{1,0:T(8,128)S(1)}, u32[]{:S(2)}, u32[]{:S(2)}) collective-permute-start(f32[256,128]{1,0:T(8,128)S(1)} %collective-permute-done.11.rest_4_), channel_id=1, source_target_pairs={{0,4},{4,0},{8,12},{12,8},{16,20},{20,16},{24,28},{28,24},{1,5},{5... | collective-permute-start | bytes 393224 | tf_op jit(solution)/shard_map/ppermute | solution.py:267
  33.2 5.0 %collective-permute-start.13 = (f32[256,128]{1,0:T(8,128)S(1)}, f32[256,128]{1,0:T(8,128)S(1)}, u32[]{:S(2)}, u32[]{:S(2)}) collective-permute-start(f32[256,128]{1,0:T(8,128)S(1)} %collective-permute-done.9.rest_2_), channel_id=1, source_target_pairs={{0,16},{4,12},{8,24},{12,4},{16,0},{20,28},{24,8},{28,20},{1,17},{... | collective-permute-start | bytes 393224 | tf_op jit(solution)/shard_map/ppermute | solution.py:267
  33.9 4.2 %collective-permute-start.10 = (f32[256,128]{1,0:T(8,128)S(1)}, f32[256,128]{1,0:T(8,128)S(1)}, u32[]{:S(2)}, u32[]{:S(2)}) collective-permute-start(f32[256,128]{1,0:T(8,128)S(1)} %collective-permute-done.9.rest_2_), channel_id=1, source_target_pairs={{0,4},{4,0},{8,12},{12,8},{16,20},{20,16},{24,28},{28,24},{1,5},{5... | collective-permute-start | bytes 393224 | tf_op jit(solution)/shard_map/ppermute | solution.py:267
  34.7 5.0 %collective-permute-start.20 = (f32[256,128]{1,0:T(8,128)S(1)}, f32[256,128]{1,0:T(8,128)S(1)}, u32[]{:S(2)}, u32[]{:S(2)}) collective-permute-start(f32[256,128]{1,0:T(8,128)S(1)} %trim.3.rest_8_), channel_id=1, source_target_pairs={{0,16},{4,12},{8,24},{12,4},{16,0},{20,28},{24,8},{28,20},{1,17},{... | collective-permute-start | bytes 393224 | tf_op jit(solution)/shard_map/ppermute | solution.py:267
  36.0 5.1 %collective-permute-start.22 = (f32[256,128]{1,0:T(8,128)S(1)}, f32[256,128]{1,0:T(8,128)S(1)}, u32[]{:S(2)}, u32[]{:S(2)}) collective-permute-start(f32[256,128]{1,0:T(8,128)S(1)} %collective-permute-done.18.rest_10_), channel_id=1, source_target_pairs={{0,16},{4,12},{8,24},{12,4},{16,0},{20,28},{24,8},{28,20},{1,17},{... | collective-permute-start | bytes 393224 | tf_op jit(solution)/shard_map/ppermute | solution.py:267
  36.7 4.3 %collective-permute-start.17 = (f32[256,128]{1,0:T(8,128)S(1)}, f32[256,128]{1,0:T(8,128)S(1)}, u32[]{:S(2)}, u32[]{:S(2)}) collective-permute-start(f32[256,128]{1,0:T(8,128)S(1)} %trim.3.rest_8_), channel_id=1, source_target_pairs={{0,4},{4,0},{8,12},{12,8},{16,20},{20,16},{24,28},{28,24},{1,5},{5... | collective-permute-start | bytes 393224 | tf_op jit(solution)/shard_map/ppermute | solution.py:267
  38.2 2.9 %collective-permute-start.19 = (f32[256,128]{1,0:T(8,128)S(1)}, f32[256,128]{1,0:T(8,128)S(1)}, u32[]{:S(2)}, u32[]{:S(2)}) collective-permute-start(f32[256,128]{1,0:T(8,128)S(1)} %collective-permute-done.18.rest_10_), channel_id=1, source_target_pairs={{0,4},{4,0},{8,12},{12,8},{16,20},{20,16},{24,28},{28,24},{1,5},{5... | collective-permute-start | bytes 393224 | tf_op jit(solution)/shard_map/ppermute | solution.py:267
  38.2 2.9 %collective-permute-start.14 = (f32[256,128]{1,0:T(8,128)S(1)}, f32[256,128]{1,0:T(8,128)S(1)}, u32[]{:S(2)}, u32[]{:S(2)}) collective-permute-start(f32[256,128]{1,0:T(8,128)S(1)} %collective-permute-done.13.rest_6_), channel_id=1, source_target_pairs={{0,4},{4,0},{8,12},{12,8},{16,20},{20,16},{24,28},{28,24},{1,5},{5... | collective-permute-start | bytes 393224 | tf_op jit(solution)/shard_map/ppermute | solution.py:267
  39.7 1.4 %collective-permute-start.21 = (f32[256,128]{1,0:T(8,128)S(1)}, f32[256,128]{1,0:T(8,128)S(1)}, u32[]{:S(2)}, u32[]{:S(2)}) collective-permute-start(f32[256,128]{1,0:T(8,128)S(1)} %collective-permute-done.20.rest_12_), channel_id=1, source_target_pairs={{0,4},{4,0},{8,12},{12,8},{16,20},{20,16},{24,28},{28,24},{1,5},{5... | collective-permute-start | bytes 393224 | tf_op jit(solution)/shard_map/ppermute | solution.py:267
  41.1 1.3 %collective-permute-start.23 = (f32[256,128]{1,0:T(8,128)S(1)}, f32[256,128]{1,0:T(8,128)S(1)}, u32[]{:S(2)}, u32[]{:S(2)}) collective-permute-start(f32[256,128]{1,0:T(8,128)S(1)} %collective-permute-done.22.rest_14_), channel_id=1, source_target_pairs={{0,4},{4,0},{8,12},{12,8},{16,20},{20,16},{24,28},{28,24},{1,5},{5... | collective-permute-start | bytes 393224 | tf_op jit(solution)/shard_map/ppermute | solution.py:267

commit v4 on v3

--- a/solution.py
+++ b/solution.py
@@ -10,6 +10,7 @@
 LANES = 128
 DEPTH = 4
 WAIT = 1
+LAST = 2
 CORES = 2
 
 
@@ -205,8 +206,8 @@
     )(weights, *blocks, *deps)
 
 
-def place_kernel(workers, rows, places, *rest):
-    blocks, (o_ref, sem) = rest[: len(places)], rest[len(places) :]
+def place_kernel(workers, rows, places, count, *rest):
+    blocks, (o_ref, sem) = rest[: len(places)], rest[count:]
     me = lax.axis_index("worker")
     copies = []
     for i, (block, (low, *route)) in enumerate(zip(blocks, places)):
@@ -218,17 +219,19 @@
         copy.wait()
 
 
-def place(blocks, workers, rows):
-    return pl.pallas_call(
-        functools.partial(place_kernel, workers, rows, list(blocks)),
+def place(blocks, workers, rows, into=()):
+    operands = [*blocks.values(), *into]
+    return pl.pallas_call(
+        functools.partial(place_kernel, workers, rows, list(blocks), len(operands)),
         out_shape=jax.ShapeDtypeStruct((workers * rows, LANES), jnp.float32),
-        in_specs=[ANY] * len(blocks),
+        in_specs=[ANY] * len(operands),
         out_specs=ANY,
         scratch_shapes=[pltpu.SemaphoreType.DMA((len(blocks),))],
+        input_output_aliases={len(blocks): 0} if into else {},
         compiler_params=pltpu.CompilerParams(vmem_limit_bytes=16 << 20),
-        cost_estimate=cost(2 * LANES * workers * rows),
+        cost_estimate=cost(2 * LANES * sum(block.shape[0] for block in blocks.values())),
         name="place",
-    )(*blocks.values())
+    )(*operands)
 
 
 def gate_kernel(*refs):
@@ -274,7 +277,11 @@
     far_chips = list(range(chips - 1, 0, -1))
     near_routes = [(label, 0) for label in range(1, chips)]
     far_routes = [(label, 1) for label in far_chips]
-    near = send_blocks(m, g, workers, near_routes, [[0, rows]] * len(near_routes), [], "near")
+    near = []
+    for group in (near_routes[:2], near_routes[2:]):
+        spans = [[0, rows]] * len(group)
+        blocks = send_blocks(m, g, workers, group, spans, near[:1], "near") if group else []
+        near += blocks
     held = [queued(block, route) for route, block in zip(near_routes, near)]
     routes = far_routes + [(0, 1), (0, 0)]
     cuts = [cut] * len(far_routes) + [[0, rows]] * 2
@@ -303,7 +310,9 @@
         for label, block in enumerate(new):
             blocks[low, label, 0] = block
             blocks[low, label, 1] = send(block, (0, 1))
-    result = place(blocks, workers, rows)
+    last = list(blocks)[-LAST:]
+    result = place({k: v for k, v in blocks.items() if k not in last}, workers, rows)
+    result = place({k: blocks[k] for k in last}, workers, rows, [result])
     return updated.reshape(momentum.shape), result.reshape(weights.shape)
 
 

time: 44 us -> 43.4 us (0.986)
  starting transfers between devices: 22.7 us -> 20.7 us
  Pallas kernels: 8.54 us -> 10.1 us
    ppermute x24, starting transfers between devices: 22.7 us -> 20.7 us  [send(): return lax.ppermute(block, 'worker', pairs)]
    pallas_call x2 -> x3, Pallas kernels: 3.23 us -> 4.13 us  [send_blocks(): pl.pallas_call(functools.partial(send_kernel, workers, routes, cuts, rows...]
    pallas_call x1 -> x2, Pallas kernels: 1.44 us -> 2.11 us  [place(): pl.pallas_call(functools.partial(place_kernel, workers, rows, list(blocks...]
  transfers between devices with their start and end apart: 24 -> 24, of which waited for: 9 -> 8; matrix products, arithmetic and copies ran while one was open for 0% -> 0% of each run, Pallas kernels for 13% -> 19%
where the time goes in v4:
time: 43.4 us; the launch traced here: 43.2 us
  starting transfers between devices  20.7 us (48%)
  waiting for transfers between devices  11.6 us (27%)
  Pallas kernels  10.1 us (23%)
  between operations  0.76 us (2%)
    ppermute x24, starting transfers between devices, send(): return lax.ppermute(block, 'worker', pairs)  20.7 us
    ppermute x24, waiting for transfers between devices, send(): return lax.ppermute(block, 'worker', pairs)  11.6 us
    pallas_call x3, Pallas kernels, send_blocks(): pl.pallas_call(functools.partial(send_kernel, workers, routes, cuts, rows...  4.13 us
    pallas_call x1, Pallas kernels, update(): pl.pallas_call(functools.partial(update_kernel, workers, pieces, rows, le...  3.37 us
    pallas_call x2, Pallas kernels, place(): pl.pallas_call(functools.partial(place_kernel, workers, rows, list(blocks...  2.11 us
  transfers between devices with their start and end apart: 24, of which 8 were waited for; matrix products, arithmetic and copies ran while one was open for 0% of the time, Pallas kernels for 19%

profile of v4, /device:TPU:0, one launch (start us, length us, event | category | flops | bytes accessed | tf_op | source)
XLA Modules:
  0.0 43.2 jit_solution(4447171515419740862)
XLA Ops:
  0.6 1.3 %near.2 = (f32[512,128]{1,0:T(8,128)S(1)}, f32[512,128]{1,0:T(8,128)S(1)}) custom-call(f32[4096,128]{1,0:T(8,128)} %bitcast.5, f32[4096,128]{1,0:T(8,128)} %bitcast.9), custom_call_target="tpu_custom_call" | custom-call | flops 393216 | bytes 1572864 | tf_op jit(solution)/shard_map/near/pallas_call | solution.py:114
  1.9 3.0 %collective-permute-start = (f32[512,128]{1,0:T(8,128)S(1)}, f32[512,128]{1,0:T(8,128)S(1)}, u32[]{:S(2)}, u32[]{:S(2)}) collective-permute-start(f32[512,128]{1,0:T(8,128)S(1)} %get-tuple-element.14.rest_0_), channel_id=1, source_target_pairs={{0,8},{4,20},{8,0},{12,28},{16,24},{20,4},{24,16},{28,12},{1,9},{5... | collective-permute-start | bytes 786440 | tf_op jit(solution)/shard_map/ppermute | solution.py:270
  4.9 1.1 %near.3 = f32[512,128]{1,0:T(8,128)S(1)} custom-call(f32[4096,128]{1,0:T(8,128)} %bitcast.6, f32[4096,128]{1,0:T(8,128)} %bitcast.10, f32[512,128]{1,0:T(8,128)S(1)} %get-tuple-element.14.rest_0_), custom_call_target="tpu_custom_call" | custom-call | flops 196608 | bytes 786432 | tf_op jit(solution)/shard_map/near/pallas_call | solution.py:114
  6.0 1.6 %collective-permute-start.2 = (f32[512,128]{1,0:T(8,128)S(1)}, f32[512,128]{1,0:T(8,128)S(1)}, u32[]{:S(2)}, u32[]{:S(2)}) collective-permute-start(f32[512,128]{1,0:T(8,128)S(1)} %near.3), channel_id=1, source_target_pairs={{0,24},{4,28},{8,16},{12,20},{16,8},{20,12},{24,0},{28,4},{1,25},{... | collective-permute-start | bytes 786440 | tf_op jit(solution)/shard_map/ppermute | solution.py:270
  7.6 0.1 collective-permute-start.1
  7.7 1.8 %far.1 = (f32[256,128]{1,0:T(8,128)S(1)}, f32[256,128]{1,0:T(8,128)S(1)}, f32[256,128]{1,0:T(8,128)S(1)}, f32[256,128]{1,0:T(8,128)S(1)}, f32[256,128]{1,0:T(8,1...) custom-call(f32[4096,128]{1,0:T(8,128)} %bitcast.7, f32[4096,128]{1,0:T(8,128)} %bitcast.11, ...), custom_call_target="tpu_custom_call" | custom-call | flops 983040 | bytes 3932160 | tf_op jit(solution)/shard_map/far/pallas_call | solution.py:114
  9.5 1.5 %collective-permute-start.5 = (f32[256,128]{1,0:T(8,128)S(1)}, f32[256,128]{1,0:T(8,128)S(1)}, u32[]{:S(2)}, u32[]{:S(2)}) collective-permute-start(f32[256,128]{1,0:T(8,128)S(1)} %get-tuple-element.15.rest_0_), channel_id=1, source_target_pairs={{0,28},{4,24},{8,20},{12,16},{16,12},{20,8},{24,4},{28,0},{1,29},{... | collective-permute-start | bytes 393224 | tf_op jit(solution)/shard_map/ppermute | solution.py:270
  11.0 1.5 %collective-permute-start.3 = (f32[512,128]{1,0:T(8,128)S(1)}, f32[512,128]{1,0:T(8,128)S(1)}, u32[]{:S(2)}, u32[]{:S(2)}) collective-permute-start(f32[512,128]{1,0:T(8,128)S(1)} %get-tuple-element.19), channel_id=1, source_target_pairs={{0,4},{4,0},{8,12},{12,8},{16,20},{20,16},{24,28},{28,24},{1,5},{5... | collective-permute-start | bytes 786440 | tf_op jit(solution)/shard_map/ppermute | solution.py:270
  12.5 3.4 %update.1 = (f32[4096,128]{1,0:T(8,128)}, f32[512,128]{1,0:T(8,128)S(1)}) custom-call(f32[4096,128]{1,0:T(8,128)} %bitcast.8, f32[4096,128]{1,0:T(8,128)} %bitcast.12, f32[4096,128]{1,0:T(8,128)} %bitcast.14, f32[256,128]{1,0:T(8,128)S(1)} %get-tuple-element.15.rest_0_), custom_call_target="tpu_custom_call" | custom-call | flops 1572864 | bytes 6291456 | tf_op jit(solution)/shard_map/update/pallas_call | solution.py:160
  15.9 0.0 collective-permute-done.refs_2_.rest_1_
  15.9 0.2 collective-permute-start.7
  16.0 2.0 %collective-permute-done.2.refs_2_.rest_3_ = f32[512,128]{1,0:T(8,128)S(1)} collective-permute-done((f32[512,128]{1,0:T(8,128)S(1)}, f32[512,128]{1,0:T(8,128)S(1)}, u32[]{:S(2)}, u32[]{:S(2)}) %collective-permute-start.2) | collective-permute-done | bytes 262176 | tf_op jit(solution)/shard_map/ppermute | solution.py:270
  18.0 0.0 collective-permute-start.4
  18.0 1.1 %collective-permute-done.1.rest_2_.refs_2_ = f32[512,128]{1,0:T(8,128)S(1)} collective-permute-done((f32[512,128]{1,0:T(8,128)S(1)}, f32[512,128]{1,0:T(8,128)S(1)}, u32[]{:S(2)}, u32[]{:S(2)}) %collective-permute-start.1) | collective-permute-done | bytes 262176 | tf_op jit(solution)/shard_map/ppermute | solution.py:270
  19.1 1.3 %collective-permute-start.12 = (f32[256,128]{1,0:T(8,128)S(1)}, f32[256,128]{1,0:T(8,128)S(1)}, u32[]{:S(2)}, u32[]{:S(2)}) collective-permute-start(f32[256,128]{1,0:T(8,128)S(1)} %gate.9), channel_id=1, source_target_pairs={{0,12},{4,16},{8,4},{12,24},{16,28},{20,0},{24,20},{28,8},{1,13},{... | collective-permute-start | bytes 393224 | tf_op jit(solution)/shard_map/ppermute | solution.py:270
  20.4 2.7 %collective-permute-done.5.refs_2_.rest_6_ = f32[256,128]{1,0:T(8,128)S(1)} collective-permute-done((f32[256,128]{1,0:T(8,128)S(1)}, f32[256,128]{1,0:T(8,128)S(1)}, u32[]{:S(2)}, u32[]{:S(2)}) %collective-permute-start.5) | collective-permute-done | bytes 131104 | tf_op jit(solution)/shard_map/ppermute | solution.py:270
  23.1 0.0 collective-permute-start.6
  23.1 2.9 %collective-permute-start.8 = (f32[256,128]{1,0:T(8,128)S(1)}, f32[256,128]{1,0:T(8,128)S(1)}, u32[]{:S(2)}, u32[]{:S(2)}) collective-permute-start(f32[256,128]{1,0:T(8,128)S(1)} %gate.8), channel_id=1, source_target_pairs={{0,12},{4,16},{8,4},{12,24},{16,28},{20,0},{24,20},{28,8},{1,13},{... | collective-permute-start | bytes 393224 | tf_op jit(solution)/shard_map/ppermute | solution.py:270
  26.0 0.0 collective-permute-done.3.rest_4_
  26.0 1.7 %collective-permute-done.4.rest_6_.rest_9_ = f32[256,128]{1,0:T(8,128)S(1)} collective-permute-done((f32[256,128]{1,0:T(8,128)S(1)}, f32[256,128]{1,0:T(8,128)S(1)}, u32[]{:S(2)}, u32[]{:S(2)}) %collective-permute-start.4) | collective-permute-done | bytes 131104 | tf_op jit(solution)/shard_map/ppermute | solution.py:270
  27.8 0.0 collective-permute-done.12.rest_8_
  27.8 0.2 trim.3.rest_0_
  28.0 0.1 collective-permute-start.16
  28.1 2.0 %collective-permute-start.14 = (f32[256,128]{1,0:T(8,128)S(1)}, f32[256,128]{1,0:T(8,128)S(1)}, u32[]{:S(2)}, u32[]{:S(2)}) collective-permute-start(f32[256,128]{1,0:T(8,128)S(1)} %trim.3.rest_0_), channel_id=1, source_target_pairs={{0,8},{4,20},{8,0},{12,28},{16,24},{20,4},{24,16},{28,12},{1,9},{5... | collective-permute-start | bytes 393224 | tf_op jit(solution)/shard_map/ppermute | solution.py:270
  30.1 0.0 collective-permute-start.13
  30.1 0.0 collective-permute-done.6.rest_7_
  30.1 0.3 trim.2.rest_8_
  30.4 1.3 %collective-permute-start.9 = (f32[256,128]{1,0:T(8,128)S(1)}, f32[256,128]{1,0:T(8,128)S(1)}, u32[]{:S(2)}, u32[]{:S(2)}) collective-permute-start(f32[256,128]{1,0:T(8,128)S(1)} %trim.2.rest_8_), channel_id=1, source_target_pairs={{0,8},{4,20},{8,0},{12,28},{16,24},{20,4},{24,16},{28,12},{1,9},{5... | collective-permute-start | bytes 393224 | tf_op jit(solution)/shard_map/ppermute | solution.py:270
  31.6 1.0 %collective-permute-start.22 = (f32[256,128]{1,0:T(8,128)S(1)}, f32[256,128]{1,0:T(8,128)S(1)}, u32[]{:S(2)}, u32[]{:S(2)}) collective-permute-start(f32[256,128]{1,0:T(8,128)S(1)} %trim.2.rest_8_), channel_id=1, source_target_pairs={{0,16},{4,12},{8,24},{12,4},{16,0},{20,28},{24,8},{28,20},{1,17},{... | collective-permute-start | bytes 393224 | tf_op jit(solution)/shard_map/ppermute | solution.py:270
  32.7 0.9 %collective-permute-done.16.rest_4_ = f32[256,128]{1,0:T(8,128)S(1)} collective-permute-done((f32[256,128]{1,0:T(8,128)S(1)}, f32[256,128]{1,0:T(8,128)S(1)}, u32[]{:S(2)}, u32[]{:S(2)}) %collective-permute-start.16) | collective-permute-done | bytes 131104 | tf_op jit(solution)/shard_map/ppermute | solution.py:270
  33.5 0.0 collective-permute-start.20
  33.5 0.0 collective-permute-done.14.rest_2_
  33.5 0.5 %collective-permute-start.17 = (f32[256,128]{1,0:T(8,128)S(1)}, f32[256,128]{1,0:T(8,128)S(1)}, u32[]{:S(2)}, u32[]{:S(2)}) collective-permute-start(f32[256,128]{1,0:T(8,128)S(1)} %collective-permute-done.16.rest_4_), channel_id=1, source_target_pairs={{0,4},{4,0},{8,12},{12,8},{16,20},{20,16},{24,28},{28,24},{1,5},{5... | collective-permute-start | bytes 393224 | tf_op jit(solution)/shard_map/ppermute | solution.py:270
  34.0 0.0 collective-permute-done.13.rest_1_
  34.0 1.0 %collective-permute-start.18 = (f32[256,128]{1,0:T(8,128)S(1)}, f32[256,128]{1,0:T(8,128)S(1)}, u32[]{:S(2)}, u32[]{:S(2)}) collective-permute-start(f32[256,128]{1,0:T(8,128)S(1)} %collective-permute-done.14.rest_2_), channel_id=1, source_target_pairs={{0,16},{4,12},{8,24},{12,4},{16,0},{20,28},{24,8},{28,20},{1,17},{... | collective-permute-start | bytes 393224 | tf_op jit(solution)/shard_map/ppermute | solution.py:270
  35.1 1.0 %collective-permute-done.9.rest_10_ = f32[256,128]{1,0:T(8,128)S(1)} collective-permute-done((f32[256,128]{1,0:T(8,128)S(1)}, f32[256,128]{1,0:T(8,128)S(1)}, u32[]{:S(2)}, u32[]{:S(2)}) %collective-permute-start.9) | collective-permute-done | bytes 131104 | tf_op jit(solution)/shard_map/ppermute | solution.py:270
  36.0 2.0 %collective-permute-start.10 = (f32[256,128]{1,0:T(8,128)S(1)}, f32[256,128]{1,0:T(8,128)S(1)}, u32[]{:S(2)}, u32[]{:S(2)}) collective-permute-start(f32[256,128]{1,0:T(8,128)S(1)} %collective-permute-done.9.rest_10_), channel_id=1, source_target_pairs={{0,16},{4,12},{8,24},{12,4},{16,0},{20,28},{24,8},{28,20},{1,17},{... | collective-permute-start | bytes 393224 | tf_op jit(solution)/shard_map/ppermute | solution.py:270
  38.1 0.0 collective-permute-done.22.rest_12_
  38.1 0.0 collective-permute-start.15
  38.1 0.0 collective-permute-done.20.rest_9_
  38.1 0.5 %collective-permute-start.21 = (f32[256,128]{1,0:T(8,128)S(1)}, f32[256,128]{1,0:T(8,128)S(1)}, u32[]{:S(2)}, u32[]{:S(2)}) collective-permute-start(f32[256,128]{1,0:T(8,128)S(1)} %collective-permute-done.9.rest_10_), channel_id=1, source_target_pairs={{0,4},{4,0},{8,12},{12,8},{16,20},{20,16},{24,28},{28,24},{1,5},{5... | collective-permute-start | bytes 393224 | tf_op jit(solution)/shard_map/ppermute | solution.py:270
  38.6 0.0 collective-permute-done.17.rest_5_
  38.6 0.1 collective-permute-start.23
  38.7 0.4 collective-permute-done.18.rest_6_
  39.0 0.1 collective-permute-start.19
  39.1 1.9 %collective-permute-done.10.rest_0_ = f32[256,128]{1,0:T(8,128)S(1)} collective-permute-done((f32[256,128]{1,0:T(8,128)S(1)}, f32[256,128]{1,0:T(8,128)S(1)}, u32[]{:S(2)}, u32[]{:S(2)}) %collective-permute-start.10) | collective-permute-done | bytes 131104 | tf_op jit(solution)/shard_map/ppermute | solution.py:270
  41.1 1.4 %place.2.rest_2_ = f32[4096,128]{1,0:T(8,128)} custom-call(f32[256,128]{1,0:T(8,128)S(1)} %trim.3.rest_0_, f32[256,128]{1,0:T(8,128)S(1)} %collective-permute-done.13.rest_1_, f32[256,128]{1,0:T(8,128)S(1)} %collective-permute-done.14.rest_2_, f32[256,128]{1,0:T(8,128)S(1)} %collective-permute-done.15.rest_3_, ...), custom_call_target="tpu_custom_call" | custom-call | flops 917504 | bytes 3670016 | tf_op jit(solution)/shard_map/place/pallas_call | solution.py:224
  42.4 0.7 %place.3 = f32[4096,128]{1,0:T(8,128)} custom-call(f32[256,128]{1,0:T(8,128)S(1)} %collective-permute-done.10.rest_0_, f32[256,128]{1,0:T(8,128)S(1)} %collective-permute-done.11.rest_1_, f32[4096,128]{1,0:T(8,128)} %place.2.rest_2_), custom_call_target="tpu_custom_call", output_to_operand_aliasing={{}: (2, {})} | custom-call | flops 131072 | bytes 524288 | tf_op jit(solution)/shard_map/place/pallas_call | solution.py:224
  (13 shorter events, 0.0 us)
Async XLA Ops:
  1.9 13.9 %collective-permute-start = (f32[512,128]{1,0:T(8,128)S(1)}, f32[512,128]{1,0:T(8,128)S(1)}, u32[]{:S(2)}, u32[]{:S(2)}) collective-permute-start(f32[512,128]{1,0:T(8,128)S(1)} %get-tuple-element.14.rest_0_), channel_id=1, source_target_pairs={{0,8},{4,20},{8,0},{12,28},{16,24},{20,4},{24,16},{28,12},{1,9},{5... | collective-permute-start | bytes 786440 | tf_op jit(solution)/shard_map/ppermute | solution.py:270
  6.0 12.0 %collective-permute-start.2 = (f32[512,128]{1,0:T(8,128)S(1)}, f32[512,128]{1,0:T(8,128)S(1)}, u32[]{:S(2)}, u32[]{:S(2)}) collective-permute-start(f32[512,128]{1,0:T(8,128)S(1)} %near.3), channel_id=1, source_target_pairs={{0,24},{4,28},{8,16},{12,20},{16,8},{20,12},{24,0},{28,4},{1,25},{... | collective-permute-start | bytes 786440 | tf_op jit(solution)/shard_map/ppermute | solution.py:270
  7.6 11.6 %collective-permute-start.1 = (f32[512,128]{1,0:T(8,128)S(1)}, f32[512,128]{1,0:T(8,128)S(1)}, u32[]{:S(2)}, u32[]{:S(2)}) collective-permute-start(f32[512,128]{1,0:T(8,128)S(1)} %get-tuple-element.18), channel_id=1, source_target_pairs={{0,16},{4,12},{8,24},{12,4},{16,0},{20,28},{24,8},{28,20},{1,17},{... | collective-permute-start | bytes 786440 | tf_op jit(solution)/shard_map/ppermute | solution.py:270
  9.5 13.6 %collective-permute-start.5 = (f32[256,128]{1,0:T(8,128)S(1)}, f32[256,128]{1,0:T(8,128)S(1)}, u32[]{:S(2)}, u32[]{:S(2)}) collective-permute-start(f32[256,128]{1,0:T(8,128)S(1)} %get-tuple-element.15.rest_0_), channel_id=1, source_target_pairs={{0,28},{4,24},{8,20},{12,16},{16,12},{20,8},{24,4},{28,0},{1,29},{... | collective-permute-start | bytes 393224 | tf_op jit(solution)/shard_map/ppermute | solution.py:270
  11.0 15.1 %collective-permute-start.3 = (f32[512,128]{1,0:T(8,128)S(1)}, f32[512,128]{1,0:T(8,128)S(1)}, u32[]{:S(2)}, u32[]{:S(2)}) collective-permute-start(f32[512,128]{1,0:T(8,128)S(1)} %get-tuple-element.19), channel_id=1, source_target_pairs={{0,4},{4,0},{8,12},{12,8},{16,20},{20,16},{24,28},{28,24},{1,5},{5... | collective-permute-start | bytes 786440 | tf_op jit(solution)/shard_map/ppermute | solution.py:270
  15.9 7.2 %collective-permute-start.7 = (f32[256,128]{1,0:T(8,128)S(1)}, f32[256,128]{1,0:T(8,128)S(1)}, u32[]{:S(2)}, u32[]{:S(2)}) collective-permute-start(f32[256,128]{1,0:T(8,128)S(1)} %gate.7), channel_id=1, source_target_pairs={{0,20},{4,8},{8,28},{12,0},{16,4},{20,24},{24,12},{28,16},{1,21},{... | collective-permute-start | bytes 393224 | tf_op jit(solution)/shard_map/ppermute | solution.py:270
  18.0 9.8 %collective-permute-start.4 = (f32[256,128]{1,0:T(8,128)S(1)}, f32[256,128]{1,0:T(8,128)S(1)}, u32[]{:S(2)}, u32[]{:S(2)}) collective-permute-start(f32[256,128]{1,0:T(8,128)S(1)} %gate.5), channel_id=1, source_target_pairs={{0,28},{4,24},{8,20},{12,16},{16,12},{20,8},{24,4},{28,0},{1,29},{... | collective-permute-start | bytes 393224 | tf_op jit(solution)/shard_map/ppermute | solution.py:270
  19.1 8.6 %collective-permute-start.12 = (f32[256,128]{1,0:T(8,128)S(1)}, f32[256,128]{1,0:T(8,128)S(1)}, u32[]{:S(2)}, u32[]{:S(2)}) collective-permute-start(f32[256,128]{1,0:T(8,128)S(1)} %gate.9), channel_id=1, source_target_pairs={{0,12},{4,16},{8,4},{12,24},{16,28},{20,0},{24,20},{28,8},{1,13},{... | collective-permute-start | bytes 393224 | tf_op jit(solution)/shard_map/ppermute | solution.py:270
  23.1 7.0 %collective-permute-start.6 = (f32[256,128]{1,0:T(8,128)S(1)}, f32[256,128]{1,0:T(8,128)S(1)}, u32[]{:S(2)}, u32[]{:S(2)}) collective-permute-start(f32[256,128]{1,0:T(8,128)S(1)} %gate.6), channel_id=1, source_target_pairs={{0,20},{4,8},{8,28},{12,0},{16,4},{20,24},{24,12},{28,16},{1,21},{... | collective-permute-start | bytes 393224 | tf_op jit(solution)/shard_map/ppermute | solution.py:270
  23.1 7.0 %collective-permute-start.8 = (f32[256,128]{1,0:T(8,128)S(1)}, f32[256,128]{1,0:T(8,128)S(1)}, u32[]{:S(2)}, u32[]{:S(2)}) collective-permute-start(f32[256,128]{1,0:T(8,128)S(1)} %gate.8), channel_id=1, source_target_pairs={{0,12},{4,16},{8,4},{12,24},{16,28},{20,0},{24,20},{28,8},{1,13},{... | collective-permute-start | bytes 393224 | tf_op jit(solution)/shard_map/ppermute | solution.py:270
  28.0 5.5 %collective-permute-start.16 = (f32[256,128]{1,0:T(8,128)S(1)}, f32[256,128]{1,0:T(8,128)S(1)}, u32[]{:S(2)}, u32[]{:S(2)}) collective-permute-start(f32[256,128]{1,0:T(8,128)S(1)} %trim.3.rest_0_), channel_id=1, source_target_pairs={{0,16},{4,12},{8,24},{12,4},{16,0},{20,28},{24,8},{28,20},{1,17},{... | collective-permute-start | bytes 393224 | tf_op jit(solution)/shard_map/ppermute | solution.py:270
  28.1 5.4 %collective-permute-start.14 = (f32[256,128]{1,0:T(8,128)S(1)}, f32[256,128]{1,0:T(8,128)S(1)}, u32[]{:S(2)}, u32[]{:S(2)}) collective-permute-start(f32[256,128]{1,0:T(8,128)S(1)} %trim.3.rest_0_), channel_id=1, source_target_pairs={{0,8},{4,20},{8,0},{12,28},{16,24},{20,4},{24,16},{28,12},{1,9},{5... | collective-permute-start | bytes 393224 | tf_op jit(solution)/shard_map/ppermute | solution.py:270
  30.1 4.0 %collective-permute-start.13 = (f32[256,128]{1,0:T(8,128)S(1)}, f32[256,128]{1,0:T(8,128)S(1)}, u32[]{:S(2)}, u32[]{:S(2)}) collective-permute-start(f32[256,128]{1,0:T(8,128)S(1)} %trim.3.rest_0_), channel_id=1, source_target_pairs={{0,4},{4,0},{8,12},{12,8},{16,20},{20,16},{24,28},{28,24},{1,5},{5... | collective-permute-start | bytes 393224 | tf_op jit(solution)/shard_map/ppermute | solution.py:270
  30.4 5.7 %collective-permute-start.9 = (f32[256,128]{1,0:T(8,128)S(1)}, f32[256,128]{1,0:T(8,128)S(1)}, u32[]{:S(2)}, u32[]{:S(2)}) collective-permute-start(f32[256,128]{1,0:T(8,128)S(1)} %trim.2.rest_8_), channel_id=1, source_target_pairs={{0,8},{4,20},{8,0},{12,28},{16,24},{20,4},{24,16},{28,12},{1,9},{5... | collective-permute-start | bytes 393224 | tf_op jit(solution)/shard_map/ppermute | solution.py:270
  31.6 6.4 %collective-permute-start.22 = (f32[256,128]{1,0:T(8,128)S(1)}, f32[256,128]{1,0:T(8,128)S(1)}, u32[]{:S(2)}, u32[]{:S(2)}) collective-permute-start(f32[256,128]{1,0:T(8,128)S(1)} %trim.2.rest_8_), channel_id=1, source_target_pairs={{0,16},{4,12},{8,24},{12,4},{16,0},{20,28},{24,8},{28,20},{1,17},{... | collective-permute-start | bytes 393224 | tf_op jit(solution)/shard_map/ppermute | solution.py:270
  33.5 4.6 %collective-permute-start.20 = (f32[256,128]{1,0:T(8,128)S(1)}, f32[256,128]{1,0:T(8,128)S(1)}, u32[]{:S(2)}, u32[]{:S(2)}) collective-permute-start(f32[256,128]{1,0:T(8,128)S(1)} %trim.2.rest_8_), channel_id=1, source_target_pairs={{0,4},{4,0},{8,12},{12,8},{16,20},{20,16},{24,28},{28,24},{1,5},{5... | collective-permute-start | bytes 393224 | tf_op jit(solution)/shard_map/ppermute | solution.py:270
  33.5 5.1 %collective-permute-start.17 = (f32[256,128]{1,0:T(8,128)S(1)}, f32[256,128]{1,0:T(8,128)S(1)}, u32[]{:S(2)}, u32[]{:S(2)}) collective-permute-start(f32[256,128]{1,0:T(8,128)S(1)} %collective-permute-done.16.rest_4_), channel_id=1, source_target_pairs={{0,4},{4,0},{8,12},{12,8},{16,20},{20,16},{24,28},{28,24},{1,5},{5... | collective-permute-start | bytes 393224 | tf_op jit(solution)/shard_map/ppermute | solution.py:270
  34.0 5.0 %collective-permute-start.18 = (f32[256,128]{1,0:T(8,128)S(1)}, f32[256,128]{1,0:T(8,128)S(1)}, u32[]{:S(2)}, u32[]{:S(2)}) collective-permute-start(f32[256,128]{1,0:T(8,128)S(1)} %collective-permute-done.14.rest_2_), channel_id=1, source_target_pairs={{0,16},{4,12},{8,24},{12,4},{16,0},{20,28},{24,8},{28,20},{1,17},{... | collective-permute-start | bytes 393224 | tf_op jit(solution)/shard_map/ppermute | solution.py:270
  36.0 5.0 %collective-permute-start.10 = (f32[256,128]{1,0:T(8,128)S(1)}, f32[256,128]{1,0:T(8,128)S(1)}, u32[]{:S(2)}, u32[]{:S(2)}) collective-permute-start(f32[256,128]{1,0:T(8,128)S(1)} %collective-permute-done.9.rest_10_), channel_id=1, source_target_pairs={{0,16},{4,12},{8,24},{12,4},{16,0},{20,28},{24,8},{28,20},{1,17},{... | collective-permute-start | bytes 393224 | tf_op jit(solution)/shard_map/ppermute | solution.py:270
  38.1 3.0 %collective-permute-start.15 = (f32[256,128]{1,0:T(8,128)S(1)}, f32[256,128]{1,0:T(8,128)S(1)}, u32[]{:S(2)}, u32[]{:S(2)}) collective-permute-start(f32[256,128]{1,0:T(8,128)S(1)} %collective-permute-done.14.rest_2_), channel_id=1, source_target_pairs={{0,4},{4,0},{8,12},{12,8},{16,20},{20,16},{24,28},{28,24},{1,5},{5... | collective-permute-start | bytes 393224 | tf_op jit(solution)/shard_map/ppermute | solution.py:270
  38.1 3.0 %collective-permute-start.21 = (f32[256,128]{1,0:T(8,128)S(1)}, f32[256,128]{1,0:T(8,128)S(1)}, u32[]{:S(2)}, u32[]{:S(2)}) collective-permute-start(f32[256,128]{1,0:T(8,128)S(1)} %collective-permute-done.9.rest_10_), channel_id=1, source_target_pairs={{0,4},{4,0},{8,12},{12,8},{16,20},{20,16},{24,28},{28,24},{1,5},{5... | collective-permute-start | bytes 393224 | tf_op jit(solution)/shard_map/ppermute | solution.py:270
  38.6 2.4 %collective-permute-start.23 = (f32[256,128]{1,0:T(8,128)S(1)}, f32[256,128]{1,0:T(8,128)S(1)}, u32[]{:S(2)}, u32[]{:S(2)}) collective-permute-start(f32[256,128]{1,0:T(8,128)S(1)} %collective-permute-done.22.rest_12_), channel_id=1, source_target_pairs={{0,4},{4,0},{8,12},{12,8},{16,20},{20,16},{24,28},{28,24},{1,5},{5... | collective-permute-start | bytes 393224 | tf_op jit(solution)/shard_map/ppermute | solution.py:270
  39.0 2.0 %collective-permute-start.19 = (f32[256,128]{1,0:T(8,128)S(1)}, f32[256,128]{1,0:T(8,128)S(1)}, u32[]{:S(2)}, u32[]{:S(2)}) collective-permute-start(f32[256,128]{1,0:T(8,128)S(1)} %collective-permute-done.18.rest_6_), channel_id=1, source_target_pairs={{0,4},{4,0},{8,12},{12,8},{16,20},{20,16},{24,28},{28,24},{1,5},{5... | collective-permute-start | bytes 393224 | tf_op jit(solution)/shard_map/ppermute | solution.py:270
  41.0 1.4 %collective-permute-start.11 = (f32[256,128]{1,0:T(8,128)S(1)}, f32[256,128]{1,0:T(8,128)S(1)}, u32[]{:S(2)}, u32[]{:S(2)}) collective-permute-start(f32[256,128]{1,0:T(8,128)S(1)} %collective-permute-done.10.rest_0_), channel_id=1, source_target_pairs={{0,4},{4,0},{8,12},{12,8},{16,20},{20,16},{24,28},{28,24},{1,5},{5... | collective-permute-start | bytes 393224 | tf_op jit(solution)/shard_map/ppermute | solution.py:270

commit v5 on v4

--- a/solution.py
+++ b/solution.py
@@ -9,6 +9,7 @@
 
 LANES = 128
 DEPTH = 4
+EARLY = 2
 WAIT = 1
 LAST = 2
 CORES = 2
@@ -291,7 +292,7 @@
     got = [[], []]
     for part in range(2):
         for i, route in enumerate(far_routes):
-            early = part == 0 and i < DEPTH - len(near_routes)
+            early = part == 0 and i < EARLY
             got[part].append(queued(sends[2 * i + part], route, *([] if early else [own_w])))
 
     gathered = []

time: 43.4 us -> 43.4 us (level)
  no operation moved by 1% of the time
where the time goes in v5:
time: 43.4 us; the launch traced here: 43.2 us
  starting transfers between devices  20.7 us (48%)
  waiting for transfers between devices  11.6 us (27%)
  Pallas kernels  10.1 us (23%)
  between operations  0.76 us (2%)
    ppermute x24, starting transfers between devices, send(): return lax.ppermute(block, 'worker', pairs)  20.7 us
    ppermute x24, waiting for transfers between devices, send(): return lax.ppermute(block, 'worker', pairs)  11.6 us
    pallas_call x3, Pallas kernels, send_blocks(): pl.pallas_call(functools.partial(send_kernel, workers, routes, cuts, rows...  4.13 us
    pallas_call x1, Pallas kernels, update(): pl.pallas_call(functools.partial(update_kernel, workers, pieces, rows, le...  3.37 us
    pallas_call x2, Pallas kernels, place(): pl.pallas_call(functools.partial(place_kernel, workers, rows, list(blocks...  2.11 us
  transfers between devices with their start and end apart: 24, of which 8 were waited for; matrix products, arithmetic and copies ran while one was open for 0% of the time, Pallas kernels for 19%

profile of v5, /device:TPU:0, one launch (start us, length us, event | category | flops | bytes accessed | tf_op | source)
XLA Modules:
  0.0 43.2 jit_solution(393716372811163909)
XLA Ops:
  0.6 1.3 %near.2 = (f32[512,128]{1,0:T(8,128)S(1)}, f32[512,128]{1,0:T(8,128)S(1)}) custom-call(f32[4096,128]{1,0:T(8,128)} %bitcast.5, f32[4096,128]{1,0:T(8,128)} %bitcast.9), custom_call_target="tpu_custom_call" | custom-call | flops 393216 | bytes 1572864 | tf_op jit(solution)/shard_map/near/pallas_call | solution.py:115
  1.9 3.0 %collective-permute-start = (f32[512,128]{1,0:T(8,128)S(1)}, f32[512,128]{1,0:T(8,128)S(1)}, u32[]{:S(2)}, u32[]{:S(2)}) collective-permute-start(f32[512,128]{1,0:T(8,128)S(1)} %get-tuple-element.14.rest_0_), channel_id=1, source_target_pairs={{0,8},{4,20},{8,0},{12,28},{16,24},{20,4},{24,16},{28,12},{1,9},{5... | collective-permute-start | bytes 786440 | tf_op jit(solution)/shard_map/ppermute | solution.py:271
  4.9 1.1 %near.3 = f32[512,128]{1,0:T(8,128)S(1)} custom-call(f32[4096,128]{1,0:T(8,128)} %bitcast.6, f32[4096,128]{1,0:T(8,128)} %bitcast.10, f32[512,128]{1,0:T(8,128)S(1)} %get-tuple-element.14.rest_0_), custom_call_target="tpu_custom_call" | custom-call | flops 196608 | bytes 786432 | tf_op jit(solution)/shard_map/near/pallas_call | solution.py:115
  6.0 1.6 %collective-permute-start.2 = (f32[512,128]{1,0:T(8,128)S(1)}, f32[512,128]{1,0:T(8,128)S(1)}, u32[]{:S(2)}, u32[]{:S(2)}) collective-permute-start(f32[512,128]{1,0:T(8,128)S(1)} %near.3), channel_id=1, source_target_pairs={{0,24},{4,28},{8,16},{12,20},{16,8},{20,12},{24,0},{28,4},{1,25},{... | collective-permute-start | bytes 786440 | tf_op jit(solution)/shard_map/ppermute | solution.py:271
  7.6 0.1 collective-permute-start.1
  7.7 1.8 %far.1 = (f32[256,128]{1,0:T(8,128)S(1)}, f32[256,128]{1,0:T(8,128)S(1)}, f32[256,128]{1,0:T(8,128)S(1)}, f32[256,128]{1,0:T(8,128)S(1)}, f32[256,128]{1,0:T(8,1...) custom-call(f32[4096,128]{1,0:T(8,128)} %bitcast.7, f32[4096,128]{1,0:T(8,128)} %bitcast.11, ...), custom_call_target="tpu_custom_call" | custom-call | flops 983040 | bytes 3932160 | tf_op jit(solution)/shard_map/far/pallas_call | solution.py:115
  9.5 0.1 collective-permute-start.3
  9.5 3.0 %collective-permute-start.5 = (f32[256,128]{1,0:T(8,128)S(1)}, f32[256,128]{1,0:T(8,128)S(1)}, u32[]{:S(2)}, u32[]{:S(2)}) collective-permute-start(f32[256,128]{1,0:T(8,128)S(1)} %get-tuple-element.15.rest_0_), channel_id=1, source_target_pairs={{0,28},{4,24},{8,20},{12,16},{16,12},{20,8},{24,4},{28,0},{1,29},{... | collective-permute-start | bytes 393224 | tf_op jit(solution)/shard_map/ppermute | solution.py:271
  12.5 0.2 collective-permute-start.7
  12.7 3.4 %update.1 = (f32[4096,128]{1,0:T(8,128)}, f32[512,128]{1,0:T(8,128)S(1)}) custom-call(f32[4096,128]{1,0:T(8,128)} %bitcast.8, f32[4096,128]{1,0:T(8,128)} %bitcast.12, f32[4096,128]{1,0:T(8,128)} %bitcast.14, f32[256,128]{1,0:T(8,128)S(1)} %get-tuple-element.15.rest_0_), custom_call_target="tpu_custom_call" | custom-call | flops 1572864 | bytes 6291456 | tf_op jit(solution)/shard_map/update/pallas_call | solution.py:161
  16.1 1.9 %collective-permute-done.2.refs_2_.rest_3_ = f32[512,128]{1,0:T(8,128)S(1)} collective-permute-done((f32[512,128]{1,0:T(8,128)S(1)}, f32[512,128]{1,0:T(8,128)S(1)}, u32[]{:S(2)}, u32[]{:S(2)}) %collective-permute-start.2) | collective-permute-done | bytes 262176 | tf_op jit(solution)/shard_map/ppermute | solution.py:271
  18.0 0.0 collective-permute-start.4
  18.0 1.1 %collective-permute-done.1.rest_2_.refs_2_ = f32[512,128]{1,0:T(8,128)S(1)} collective-permute-done((f32[512,128]{1,0:T(8,128)S(1)}, f32[512,128]{1,0:T(8,128)S(1)}, u32[]{:S(2)}, u32[]{:S(2)}) %collective-permute-start.1) | collective-permute-done | bytes 262176 | tf_op jit(solution)/shard_map/ppermute | solution.py:271
  19.1 1.3 %collective-permute-start.12 = (f32[256,128]{1,0:T(8,128)S(1)}, f32[256,128]{1,0:T(8,128)S(1)}, u32[]{:S(2)}, u32[]{:S(2)}) collective-permute-start(f32[256,128]{1,0:T(8,128)S(1)} %gate.9), channel_id=1, source_target_pairs={{0,12},{4,16},{8,4},{12,24},{16,28},{20,0},{24,20},{28,8},{1,13},{... | collective-permute-start | bytes 393224 | tf_op jit(solution)/shard_map/ppermute | solution.py:271
  20.4 2.7 %collective-permute-done.5.refs_2_.rest_6_ = f32[256,128]{1,0:T(8,128)S(1)} collective-permute-done((f32[256,128]{1,0:T(8,128)S(1)}, f32[256,128]{1,0:T(8,128)S(1)}, u32[]{:S(2)}, u32[]{:S(2)}) %collective-permute-start.5) | collective-permute-done | bytes 131104 | tf_op jit(solution)/shard_map/ppermute | solution.py:271
  23.1 0.0 collective-permute-start.6
  23.1 2.9 %collective-permute-start.8 = (f32[256,128]{1,0:T(8,128)S(1)}, f32[256,128]{1,0:T(8,128)S(1)}, u32[]{:S(2)}, u32[]{:S(2)}) collective-permute-start(f32[256,128]{1,0:T(8,128)S(1)} %gate.8), channel_id=1, source_target_pairs={{0,12},{4,16},{8,4},{12,24},{16,28},{20,0},{24,20},{28,8},{1,13},{... | collective-permute-start | bytes 393224 | tf_op jit(solution)/shard_map/ppermute | solution.py:271
  26.0 0.0 collective-permute-done.3.rest_4_
  26.0 1.7 %collective-permute-done.4.rest_6_.rest_9_ = f32[256,128]{1,0:T(8,128)S(1)} collective-permute-done((f32[256,128]{1,0:T(8,128)S(1)}, f32[256,128]{1,0:T(8,128)S(1)}, u32[]{:S(2)}, u32[]{:S(2)}) %collective-permute-start.4) | collective-permute-done | bytes 131104 | tf_op jit(solution)/shard_map/ppermute | solution.py:271
  27.8 0.0 collective-permute-done.12.rest_8_
  27.8 0.2 trim.3.rest_0_
  28.0 0.1 collective-permute-start.16
  28.1 2.0 %collective-permute-start.14 = (f32[256,128]{1,0:T(8,128)S(1)}, f32[256,128]{1,0:T(8,128)S(1)}, u32[]{:S(2)}, u32[]{:S(2)}) collective-permute-start(f32[256,128]{1,0:T(8,128)S(1)} %trim.3.rest_0_), channel_id=1, source_target_pairs={{0,8},{4,20},{8,0},{12,28},{16,24},{20,4},{24,16},{28,12},{1,9},{5... | collective-permute-start | bytes 393224 | tf_op jit(solution)/shard_map/ppermute | solution.py:271
  30.1 0.0 collective-permute-start.13
  30.1 0.0 collective-permute-done.6.rest_7_
  30.1 0.3 trim.2.rest_8_
  30.4 1.3 %collective-permute-start.9 = (f32[256,128]{1,0:T(8,128)S(1)}, f32[256,128]{1,0:T(8,128)S(1)}, u32[]{:S(2)}, u32[]{:S(2)}) collective-permute-start(f32[256,128]{1,0:T(8,128)S(1)} %trim.2.rest_8_), channel_id=1, source_target_pairs={{0,8},{4,20},{8,0},{12,28},{16,24},{20,4},{24,16},{28,12},{1,9},{5... | collective-permute-start | bytes 393224 | tf_op jit(solution)/shard_map/ppermute | solution.py:271
  31.6 1.0 %collective-permute-start.22 = (f32[256,128]{1,0:T(8,128)S(1)}, f32[256,128]{1,0:T(8,128)S(1)}, u32[]{:S(2)}, u32[]{:S(2)}) collective-permute-start(f32[256,128]{1,0:T(8,128)S(1)} %trim.2.rest_8_), channel_id=1, source_target_pairs={{0,16},{4,12},{8,24},{12,4},{16,0},{20,28},{24,8},{28,20},{1,17},{... | collective-permute-start | bytes 393224 | tf_op jit(solution)/shard_map/ppermute | solution.py:271
  32.7 0.9 %collective-permute-done.16.rest_4_ = f32[256,128]{1,0:T(8,128)S(1)} collective-permute-done((f32[256,128]{1,0:T(8,128)S(1)}, f32[256,128]{1,0:T(8,128)S(1)}, u32[]{:S(2)}, u32[]{:S(2)}) %collective-permute-start.16) | collective-permute-done | bytes 131104 | tf_op jit(solution)/shard_map/ppermute | solution.py:271
  33.5 0.0 collective-permute-start.20
  33.5 0.0 collective-permute-done.14.rest_2_
  33.5 0.5 %collective-permute-start.17 = (f32[256,128]{1,0:T(8,128)S(1)}, f32[256,128]{1,0:T(8,128)S(1)}, u32[]{:S(2)}, u32[]{:S(2)}) collective-permute-start(f32[256,128]{1,0:T(8,128)S(1)} %collective-permute-done.16.rest_4_), channel_id=1, source_target_pairs={{0,4},{4,0},{8,12},{12,8},{16,20},{20,16},{24,28},{28,24},{1,5},{5... | collective-permute-start | bytes 393224 | tf_op jit(solution)/shard_map/ppermute | solution.py:271
  34.0 0.0 collective-permute-done.13.rest_1_
  34.0 1.0 %collective-permute-start.18 = (f32[256,128]{1,0:T(8,128)S(1)}, f32[256,128]{1,0:T(8,128)S(1)}, u32[]{:S(2)}, u32[]{:S(2)}) collective-permute-start(f32[256,128]{1,0:T(8,128)S(1)} %collective-permute-done.14.rest_2_), channel_id=1, source_target_pairs={{0,16},{4,12},{8,24},{12,4},{16,0},{20,28},{24,8},{28,20},{1,17},{... | collective-permute-start | bytes 393224 | tf_op jit(solution)/shard_map/ppermute | solution.py:271
  35.1 1.0 %collective-permute-done.9.rest_10_ = f32[256,128]{1,0:T(8,128)S(1)} collective-permute-done((f32[256,128]{1,0:T(8,128)S(1)}, f32[256,128]{1,0:T(8,128)S(1)}, u32[]{:S(2)}, u32[]{:S(2)}) %collective-permute-start.9) | collective-permute-done | bytes 131104 | tf_op jit(solution)/shard_map/ppermute | solution.py:271
  36.0 2.0 %collective-permute-start.10 = (f32[256,128]{1,0:T(8,128)S(1)}, f32[256,128]{1,0:T(8,128)S(1)}, u32[]{:S(2)}, u32[]{:S(2)}) collective-permute-start(f32[256,128]{1,0:T(8,128)S(1)} %collective-permute-done.9.rest_10_), channel_id=1, source_target_pairs={{0,16},{4,12},{8,24},{12,4},{16,0},{20,28},{24,8},{28,20},{1,17},{... | collective-permute-start | bytes 393224 | tf_op jit(solution)/shard_map/ppermute | solution.py:271
  38.1 0.0 collective-permute-done.22.rest_12_
  38.1 0.0 collective-permute-start.15
  38.1 0.0 collective-permute-done.20.rest_9_
  38.1 0.5 %collective-permute-start.21 = (f32[256,128]{1,0:T(8,128)S(1)}, f32[256,128]{1,0:T(8,128)S(1)}, u32[]{:S(2)}, u32[]{:S(2)}) collective-permute-start(f32[256,128]{1,0:T(8,128)S(1)} %collective-permute-done.9.rest_10_), channel_id=1, source_target_pairs={{0,4},{4,0},{8,12},{12,8},{16,20},{20,16},{24,28},{28,24},{1,5},{5... | collective-permute-start | bytes 393224 | tf_op jit(solution)/shard_map/ppermute | solution.py:271
  38.6 0.0 collective-permute-done.17.rest_5_
  38.6 0.1 collective-permute-start.23
  38.7 0.4 collective-permute-done.18.rest_6_
  39.0 0.1 collective-permute-start.19
  39.1 1.9 %collective-permute-done.10.rest_0_ = f32[256,128]{1,0:T(8,128)S(1)} collective-permute-done((f32[256,128]{1,0:T(8,128)S(1)}, f32[256,128]{1,0:T(8,128)S(1)}, u32[]{:S(2)}, u32[]{:S(2)}) %collective-permute-start.10) | collective-permute-done | bytes 131104 | tf_op jit(solution)/shard_map/ppermute | solution.py:271
  41.0 0.0 collective-permute-start.11
  41.1 1.4 %place.2.rest_2_ = f32[4096,128]{1,0:T(8,128)} custom-call(f32[256,128]{1,0:T(8,128)S(1)} %trim.3.rest_0_, f32[256,128]{1,0:T(8,128)S(1)} %collective-permute-done.13.rest_1_, f32[256,128]{1,0:T(8,128)S(1)} %collective-permute-done.14.rest_2_, f32[256,128]{1,0:T(8,128)S(1)} %collective-permute-done.15.rest_3_, ...), custom_call_target="tpu_custom_call" | custom-call | flops 917504 | bytes 3670016 | tf_op jit(solution)/shard_map/place/pallas_call | solution.py:225
  42.4 0.7 %place.3 = f32[4096,128]{1,0:T(8,128)} custom-call(f32[256,128]{1,0:T(8,128)S(1)} %collective-permute-done.10.rest_0_, f32[256,128]{1,0:T(8,128)S(1)} %collective-permute-done.11.rest_1_, f32[4096,128]{1,0:T(8,128)} %place.2.rest_2_), custom_call_target="tpu_custom_call", output_to_operand_aliasing={{}: (2, {})} | custom-call | flops 131072 | bytes 524288 | tf_op jit(solution)/shard_map/place/pallas_call | solution.py:225
  (13 shorter events, 0.0 us)
Async XLA Ops:
  1.9 10.6 %collective-permute-start = (f32[512,128]{1,0:T(8,128)S(1)}, f32[512,128]{1,0:T(8,128)S(1)}, u32[]{:S(2)}, u32[]{:S(2)}) collective-permute-start(f32[512,128]{1,0:T(8,128)S(1)} %get-tuple-element.14.rest_0_), channel_id=1, source_target_pairs={{0,8},{4,20},{8,0},{12,28},{16,24},{20,4},{24,16},{28,12},{1,9},{5... | collective-permute-start | bytes 786440 | tf_op jit(solution)/shard_map/ppermute | solution.py:271
  6.0 12.0 %collective-permute-start.2 = (f32[512,128]{1,0:T(8,128)S(1)}, f32[512,128]{1,0:T(8,128)S(1)}, u32[]{:S(2)}, u32[]{:S(2)}) collective-permute-start(f32[512,128]{1,0:T(8,128)S(1)} %near.3), channel_id=1, source_target_pairs={{0,24},{4,28},{8,16},{12,20},{16,8},{20,12},{24,0},{28,4},{1,25},{... | collective-permute-start | bytes 786440 | tf_op jit(solution)/shard_map/ppermute | solution.py:271
  7.6 11.6 %collective-permute-start.1 = (f32[512,128]{1,0:T(8,128)S(1)}, f32[512,128]{1,0:T(8,128)S(1)}, u32[]{:S(2)}, u32[]{:S(2)}) collective-permute-start(f32[512,128]{1,0:T(8,128)S(1)} %get-tuple-element.18), channel_id=1, source_target_pairs={{0,16},{4,12},{8,24},{12,4},{16,0},{20,28},{24,8},{28,20},{1,17},{... | collective-permute-start | bytes 786440 | tf_op jit(solution)/shard_map/ppermute | solution.py:271
  9.5 16.6 %collective-permute-start.3 = (f32[512,128]{1,0:T(8,128)S(1)}, f32[512,128]{1,0:T(8,128)S(1)}, u32[]{:S(2)}, u32[]{:S(2)}) collective-permute-start(f32[512,128]{1,0:T(8,128)S(1)} %get-tuple-element.19), channel_id=1, source_target_pairs={{0,4},{4,0},{8,12},{12,8},{16,20},{20,16},{24,28},{28,24},{1,5},{5... | collective-permute-start | bytes 786440 | tf_op jit(solution)/shard_map/ppermute | solution.py:271
  9.5 13.5 %collective-permute-start.5 = (f32[256,128]{1,0:T(8,128)S(1)}, f32[256,128]{1,0:T(8,128)S(1)}, u32[]{:S(2)}, u32[]{:S(2)}) collective-permute-start(f32[256,128]{1,0:T(8,128)S(1)} %get-tuple-element.15.rest_0_), channel_id=1, source_target_pairs={{0,28},{4,24},{8,20},{12,16},{16,12},{20,8},{24,4},{28,0},{1,29},{... | collective-permute-start | bytes 393224 | tf_op jit(solution)/shard_map/ppermute | solution.py:271
  12.5 10.6 %collective-permute-start.7 = (f32[256,128]{1,0:T(8,128)S(1)}, f32[256,128]{1,0:T(8,128)S(1)}, u32[]{:S(2)}, u32[]{:S(2)}) collective-permute-start(f32[256,128]{1,0:T(8,128)S(1)} %gate.7), channel_id=1, source_target_pairs={{0,20},{4,8},{8,28},{12,0},{16,4},{20,24},{24,12},{28,16},{1,21},{... | collective-permute-start | bytes 393224 | tf_op jit(solution)/shard_map/ppermute | solution.py:271
  18.0 9.8 %collective-permute-start.4 = (f32[256,128]{1,0:T(8,128)S(1)}, f32[256,128]{1,0:T(8,128)S(1)}, u32[]{:S(2)}, u32[]{:S(2)}) collective-permute-start(f32[256,128]{1,0:T(8,128)S(1)} %gate.5), channel_id=1, source_target_pairs={{0,28},{4,24},{8,20},{12,16},{16,12},{20,8},{24,4},{28,0},{1,29},{... | collective-permute-start | bytes 393224 | tf_op jit(solution)/shard_map/ppermute | solution.py:271
  19.1 8.6 %collective-permute-start.12 = (f32[256,128]{1,0:T(8,128)S(1)}, f32[256,128]{1,0:T(8,128)S(1)}, u32[]{:S(2)}, u32[]{:S(2)}) collective-permute-start(f32[256,128]{1,0:T(8,128)S(1)} %gate.9), channel_id=1, source_target_pairs={{0,12},{4,16},{8,4},{12,24},{16,28},{20,0},{24,20},{28,8},{1,13},{... | collective-permute-start | bytes 393224 | tf_op jit(solution)/shard_map/ppermute | solution.py:271
  23.1 7.0 %collective-permute-start.6 = (f32[256,128]{1,0:T(8,128)S(1)}, f32[256,128]{1,0:T(8,128)S(1)}, u32[]{:S(2)}, u32[]{:S(2)}) collective-permute-start(f32[256,128]{1,0:T(8,128)S(1)} %gate.6), channel_id=1, source_target_pairs={{0,20},{4,8},{8,28},{12,0},{16,4},{20,24},{24,12},{28,16},{1,21},{... | collective-permute-start | bytes 393224 | tf_op jit(solution)/shard_map/ppermute | solution.py:271
  23.1 7.0 %collective-permute-start.8 = (f32[256,128]{1,0:T(8,128)S(1)}, f32[256,128]{1,0:T(8,128)S(1)}, u32[]{:S(2)}, u32[]{:S(2)}) collective-permute-start(f32[256,128]{1,0:T(8,128)S(1)} %gate.8), channel_id=1, source_target_pairs={{0,12},{4,16},{8,4},{12,24},{16,28},{20,0},{24,20},{28,8},{1,13},{... | collective-permute-start | bytes 393224 | tf_op jit(solution)/shard_map/ppermute | solution.py:271
  28.0 5.5 %collective-permute-start.16 = (f32[256,128]{1,0:T(8,128)S(1)}, f32[256,128]{1,0:T(8,128)S(1)}, u32[]{:S(2)}, u32[]{:S(2)}) collective-permute-start(f32[256,128]{1,0:T(8,128)S(1)} %trim.3.rest_0_), channel_id=1, source_target_pairs={{0,16},{4,12},{8,24},{12,4},{16,0},{20,28},{24,8},{28,20},{1,17},{... | collective-permute-start | bytes 393224 | tf_op jit(solution)/shard_map/ppermute | solution.py:271
  28.1 5.4 %collective-permute-start.14 = (f32[256,128]{1,0:T(8,128)S(1)}, f32[256,128]{1,0:T(8,128)S(1)}, u32[]{:S(2)}, u32[]{:S(2)}) collective-permute-start(f32[256,128]{1,0:T(8,128)S(1)} %trim.3.rest_0_), channel_id=1, source_target_pairs={{0,8},{4,20},{8,0},{12,28},{16,24},{20,4},{24,16},{28,12},{1,9},{5... | collective-permute-start | bytes 393224 | tf_op jit(solution)/shard_map/ppermute | solution.py:271
  30.1 4.0 %collective-permute-start.13 = (f32[256,128]{1,0:T(8,128)S(1)}, f32[256,128]{1,0:T(8,128)S(1)}, u32[]{:S(2)}, u32[]{:S(2)}) collective-permute-start(f32[256,128]{1,0:T(8,128)S(1)} %trim.3.rest_0_), channel_id=1, source_target_pairs={{0,4},{4,0},{8,12},{12,8},{16,20},{20,16},{24,28},{28,24},{1,5},{5... | collective-permute-start | bytes 393224 | tf_op jit(solution)/shard_map/ppermute | solution.py:271
  30.4 5.7 %collective-permute-start.9 = (f32[256,128]{1,0:T(8,128)S(1)}, f32[256,128]{1,0:T(8,128)S(1)}, u32[]{:S(2)}, u32[]{:S(2)}) collective-permute-start(f32[256,128]{1,0:T(8,128)S(1)} %trim.2.rest_8_), channel_id=1, source_target_pairs={{0,8},{4,20},{8,0},{12,28},{16,24},{20,4},{24,16},{28,12},{1,9},{5... | collective-permute-start | bytes 393224 | tf_op jit(solution)/shard_map/ppermute | solution.py:271
  31.6 6.4 %collective-permute-start.22 = (f32[256,128]{1,0:T(8,128)S(1)}, f32[256,128]{1,0:T(8,128)S(1)}, u32[]{:S(2)}, u32[]{:S(2)}) collective-permute-start(f32[256,128]{1,0:T(8,128)S(1)} %trim.2.rest_8_), channel_id=1, source_target_pairs={{0,16},{4,12},{8,24},{12,4},{16,0},{20,28},{24,8},{28,20},{1,17},{... | collective-permute-start | bytes 393224 | tf_op jit(solution)/shard_map/ppermute | solution.py:271
  33.5 4.6 %collective-permute-start.20 = (f32[256,128]{1,0:T(8,128)S(1)}, f32[256,128]{1,0:T(8,128)S(1)}, u32[]{:S(2)}, u32[]{:S(2)}) collective-permute-start(f32[256,128]{1,0:T(8,128)S(1)} %trim.2.rest_8_), channel_id=1, source_target_pairs={{0,4},{4,0},{8,12},{12,8},{16,20},{20,16},{24,28},{28,24},{1,5},{5... | collective-permute-start | bytes 393224 | tf_op jit(solution)/shard_map/ppermute | solution.py:271
  33.5 5.1 %collective-permute-start.17 = (f32[256,128]{1,0:T(8,128)S(1)}, f32[256,128]{1,0:T(8,128)S(1)}, u32[]{:S(2)}, u32[]{:S(2)}) collective-permute-start(f32[256,128]{1,0:T(8,128)S(1)} %collective-permute-done.16.rest_4_), channel_id=1, source_target_pairs={{0,4},{4,0},{8,12},{12,8},{16,20},{20,16},{24,28},{28,24},{1,5},{5... | collective-permute-start | bytes 393224 | tf_op jit(solution)/shard_map/ppermute | solution.py:271
  34.0 5.0 %collective-permute-start.18 = (f32[256,128]{1,0:T(8,128)S(1)}, f32[256,128]{1,0:T(8,128)S(1)}, u32[]{:S(2)}, u32[]{:S(2)}) collective-permute-start(f32[256,128]{1,0:T(8,128)S(1)} %collective-permute-done.14.rest_2_), channel_id=1, source_target_pairs={{0,16},{4,12},{8,24},{12,4},{16,0},{20,28},{24,8},{28,20},{1,17},{... | collective-permute-start | bytes 393224 | tf_op jit(solution)/shard_map/ppermute | solution.py:271
  36.0 5.0 %collective-permute-start.10 = (f32[256,128]{1,0:T(8,128)S(1)}, f32[256,128]{1,0:T(8,128)S(1)}, u32[]{:S(2)}, u32[]{:S(2)}) collective-permute-start(f32[256,128]{1,0:T(8,128)S(1)} %collective-permute-done.9.rest_10_), channel_id=1, source_target_pairs={{0,16},{4,12},{8,24},{12,4},{16,0},{20,28},{24,8},{28,20},{1,17},{... | collective-permute-start | bytes 393224 | tf_op jit(solution)/shard_map/ppermute | solution.py:271
  38.1 3.0 %collective-permute-start.15 = (f32[256,128]{1,0:T(8,128)S(1)}, f32[256,128]{1,0:T(8,128)S(1)}, u32[]{:S(2)}, u32[]{:S(2)}) collective-permute-start(f32[256,128]{1,0:T(8,128)S(1)} %collective-permute-done.14.rest_2_), channel_id=1, source_target_pairs={{0,4},{4,0},{8,12},{12,8},{16,20},{20,16},{24,28},{28,24},{1,5},{5... | collective-permute-start | bytes 393224 | tf_op jit(solution)/shard_map/ppermute | solution.py:271
  38.1 3.0 %collective-permute-start.21 = (f32[256,128]{1,0:T(8,128)S(1)}, f32[256,128]{1,0:T(8,128)S(1)}, u32[]{:S(2)}, u32[]{:S(2)}) collective-permute-start(f32[256,128]{1,0:T(8,128)S(1)} %collective-permute-done.9.rest_10_), channel_id=1, source_target_pairs={{0,4},{4,0},{8,12},{12,8},{16,20},{20,16},{24,28},{28,24},{1,5},{5... | collective-permute-start | bytes 393224 | tf_op jit(solution)/shard_map/ppermute | solution.py:271
  38.6 2.4 %collective-permute-start.23 = (f32[256,128]{1,0:T(8,128)S(1)}, f32[256,128]{1,0:T(8,128)S(1)}, u32[]{:S(2)}, u32[]{:S(2)}) collective-permute-start(f32[256,128]{1,0:T(8,128)S(1)} %collective-permute-done.22.rest_12_), channel_id=1, source_target_pairs={{0,4},{4,0},{8,12},{12,8},{16,20},{20,16},{24,28},{28,24},{1,5},{5... | collective-permute-start | bytes 393224 | tf_op jit(solution)/shard_map/ppermute | solution.py:271
  39.0 2.0 %collective-permute-start.19 = (f32[256,128]{1,0:T(8,128)S(1)}, f32[256,128]{1,0:T(8,128)S(1)}, u32[]{:S(2)}, u32[]{:S(2)}) collective-permute-start(f32[256,128]{1,0:T(8,128)S(1)} %collective-permute-done.18.rest_6_), channel_id=1, source_target_pairs={{0,4},{4,0},{8,12},{12,8},{16,20},{20,16},{24,28},{28,24},{1,5},{5... | collective-permute-start | bytes 393224 | tf_op jit(solution)/shard_map/ppermute | solution.py:271
  41.0 1.4 %collective-permute-start.11 = (f32[256,128]{1,0:T(8,128)S(1)}, f32[256,128]{1,0:T(8,128)S(1)}, u32[]{:S(2)}, u32[]{:S(2)}) collective-permute-start(f32[256,128]{1,0:T(8,128)S(1)} %collective-permute-done.10.rest_0_), channel_id=1, source_target_pairs={{0,4},{4,0},{8,12},{12,8},{16,20},{20,16},{24,28},{28,24},{1,5},{5... | collective-permute-start | bytes 393224 | tf_op jit(solution)/shard_map/ppermute | solution.py:271
